TPU v7x, 32 devices: a whole 2x2x4 slice. The times are simulated.
32 devices in a mesh: gx: 2 (over x), ta: 4 (over y, core), gy: 4 (over z).
Axes of the slice: x: 2, y: 2, z: 4, core: 2. Of those that a mesh axis runs over, the one named last changes fastest.
Arguments:
- initial_field: float32 [22, 20, 5, 128], P('gx', 'gy'), may hold values from -6 to 6
- opening_guess: float32 [4, 22, 20, 5, 128], P('ta', 'gx', 'gy'), may hold values from -6 to 6
- conductivity: float32 [22, 20, 5, 128], P('gx', 'gy'), may hold values from 0.5 to 2
- capacity: float32 [22, 20, 5, 128], P('gx', 'gy'), may hold values from 0.5 to 2
- section_count: int32 [2], P('gx'), may hold values from 3 to 4, as said below
Outputs:
- block_end: float32 [4, 22, 20, 5, 128], P('ta', 'gx', 'gy')
- robin_next: float32 [2, 2, 4, 20, 5, 128], P('gx', None, 'ta', 'gy')
Inputs may be any that keep to these rules, and one draw needn't show every extreme that they name: `section_count`: some subdomain takes 3 sections and some takes 4.
All inputs are finite; a program needn't handle non-finite values.
Results may differ from a plain program's by a relative error of at most 0.0003.
Values sent between devices are 32-bit elements; how exact they have to be, the bound alone decides.
A program may use at most 64 MiB of HBM per device.

v0:
```python
import math

import jax
import jax.numpy as jnp
import numpy as np
from jax import lax
from jax.sharding import PartitionSpec as P

STEPS = 1
ITERS = 2
SMIN = 3
SMAX = 4


robin_gain = 2.0
kappa_top = 2.0
capacity_low = 0.5
damping = 0.05
highest = lax.Precision.HIGHEST


def shifted_2(value, axis, steps):
    count = lax.axis_size(axis)
    pairs = [(source, (source + steps) % count) for source in range(count)]
    return lax.ppermute(value, axis, pairs)


def shifted_3(value, axis, steps):
    count = lax.axis_size(axis)
    leading, last = (max(0, -steps), min(count, count - steps))
    return lax.ppermute(value, axis, [(source, source + steps) for source in range(leading, last)])


def gll_tables():
    root_seven = math.sqrt(7.0)
    outer = math.sqrt(1.0 / 3.0 + 2.0 * root_seven / 21.0)
    closer = math.sqrt(1.0 / 3.0 - 2.0 * root_seven / 21.0)
    points = np.array([-1.0, -outer, -closer, closer, outer, 1.0])
    weights = np.array(
        [
            1.0 / 15.0,
            (14.0 - root_seven) / 30.0,
            (14.0 + root_seven) / 30.0,
            (14.0 + root_seven) / 30.0,
            (14.0 - root_seven) / 30.0,
            1.0 / 15.0,
        ]
    )
    products = np.array(
        [np.prod([points[i] - points[k] for k in range(6) if k != i]) for i in range(6)]
    )
    derivative = np.zeros((6, 6))
    for i in range(6):
        for k in range(6):
            if i != k:
                derivative[i, k] = products[i] / (products[k] * (points[i] - points[k]))
    for i in range(6):
        derivative[i, i] = -derivative[i].sum()
    return (points, weights, derivative)


def line_weights(count, closed):
    weights = gll_tables()[1]
    pattern = np.array([weights[i % 5] if i % 5 else 2.0 * weights[0] for i in range(count)])
    if closed:
        pattern[0] = weights[0]
        pattern[-1] = weights[0]
    return pattern


def step_size():
    points, weights, derivative = gll_tables()
    row_sums = np.abs(derivative).sum(axis=1)
    gersh_bound = max(
        (
            float(np.sum(np.abs(derivative[:, i]) * weights * row_sums) / weights[i])
            for i in range(6)
        )
    )
    spectral = kappa_top / capacity_low * 3.0 * gersh_bound + robin_gain / (
        capacity_low * weights[0]
    )
    return float(0.8 * 1.93 * SMIN**2 / spectral)


def rkc_table(sections):
    section_real = sections.astype(jnp.float32)
    shifted = 1.0 + damping / (section_real * section_real)
    chebyshev = [jnp.ones((), jnp.float32), shifted]
    derivs = [jnp.zeros((), jnp.float32), jnp.ones((), jnp.float32)]
    for section in range(2, SMAX + 1):
        chebyshev.append(2.0 * shifted * chebyshev[-1] - chebyshev[-2])
        derivs.append(
            2.0 * chebyshev[section - 1] + 2.0 * shifted * derivs[section - 1] - derivs[section - 2]
        )
    cheb_end = jnp.zeros((), jnp.float32)
    slope_end = jnp.zeros((), jnp.float32)
    for section in range(SMIN, SMAX + 1):
        cheb_end = jnp.where(sections == section, chebyshev[section], cheb_end)
        slope_end = jnp.where(sections == section, derivs[section], slope_end)
    spread = cheb_end / slope_end
    coef_mu = [0.0, 0.0] + [
        2.0 * shifted * chebyshev[j - 1] / chebyshev[j] for j in range(2, SMAX + 1)
    ]
    coef_nu = [0.0, 0.0] + [-chebyshev[j - 2] / chebyshev[j] for j in range(2, SMAX + 1)]
    coef_tilde = [0.0, 0.0] + [
        2.0 * spread * chebyshev[j - 1] / chebyshev[j] for j in range(2, SMAX + 1)
    ]
    return (spread / shifted, coef_mu, coef_nu, coef_tilde)


def along_first(field):
    element_count = (field.shape[0] - 1) // 5
    leading = field[:-1].reshape((element_count, 5) + field.shape[1:])
    return jnp.concatenate([leading, field[5::5][:, None]], axis=1)


def terms_first(field, tables):
    derivative, quad, kappa_x = (tables["derivative"], tables["quad"], tables["kappa_x"])
    element = along_first(field)
    slopes = jnp.einsum("ab,eb...->ea...", derivative, element, precision=highest)
    flux = slopes * kappa_x * quad[None, :, None, None, None] * tables["scale_x"][None, None]
    returned = jnp.einsum("ab,ea...->eb...", derivative, flux, precision=highest)
    leading = returned[:, :5]
    carried = jnp.concatenate([jnp.zeros_like(returned[:1, 5]), returned[:-1, 5]], axis=0)
    leading = leading.at[:, 0].add(carried)
    element_count = leading.shape[0]
    return jnp.concatenate(
        [leading.reshape((5 * element_count,) + field.shape[1:]), returned[-1:, 5]], axis=0
    )


def along_second(extended):
    element_count = (extended.shape[1] - 1) // 5
    leading = extended[:, :-1].reshape((extended.shape[0], element_count, 5) + extended.shape[2:])
    return jnp.concatenate([leading, extended[:, 5::5][:, :, None]], axis=2)


def terms_second(extended, kappa_y, tables):
    derivative, quad = (tables["derivative"], tables["quad"])
    element = along_second(extended)
    slopes = jnp.einsum("ab,xeb...->xea...", derivative, element, precision=highest)
    flux = slopes * kappa_y * quad[None, None, :, None, None] * tables["scale_y"]
    returned = jnp.einsum("ab,xea...->xeb...", derivative, flux, precision=highest)
    leading = returned[:, :, :5]
    carried = jnp.concatenate([jnp.zeros_like(returned[:, :1, 5]), returned[:, :-1, 5]], axis=1)
    leading = leading.at[:, :, 0].add(carried)
    shape = leading.shape
    interior = leading.reshape((shape[0], shape[1] * 5) + shape[3:])
    return (interior, returned[:, -1, 5])


def along_third(field):
    return jnp.concatenate([field, jnp.roll(field[:, :, :1], -1, axis=3)], axis=2)


def terms_third(field, tables):
    derivative, quad = (tables["derivative"], tables["quad"])
    element = along_third(field)
    slopes = jnp.einsum("ab,xybe->xyae", derivative, element, precision=highest)
    flux = slopes * tables["kappa_z"] * quad[:, None] * tables["scale_z"]
    returned = jnp.einsum("ab,xyae->xybe", derivative, flux, precision=highest)
    leading = returned[:, :, :5]
    return leading.at[:, :, 0].add(jnp.roll(returned[:, :, 5], 1, axis=-1))


def build_tables(conductivity, capacity):
    points, weights, derivative = gll_tables()
    weight_x = jnp.asarray(line_weights(conductivity.shape[0], True), jnp.float32)
    weight_y = jnp.asarray(line_weights(conductivity.shape[1], False), jnp.float32)
    weight_z = jnp.asarray(line_weights(5, False), jnp.float32)
    return {
        "derivative": jnp.asarray(derivative, jnp.float32),
        "quad": jnp.asarray(weights, jnp.float32),
        "kappa_x": along_first(conductivity),
        "kappa_z": along_third(conductivity),
        "scale_x": (weight_y[:, None] * weight_z[None, :])[:, :, None],
        "scale_y": (weight_x[:, None] * weight_z[None, :])[:, None, None, :, None],
        "scale_z": (weight_x[:, None] * weight_y[None, :])[:, :, None, None],
        "face_weight": (weight_y[:, None] * weight_z[None, :])[:, :, None],
        "lumped": capacity
        * weight_x[:, None, None, None]
        * weight_y[None, :, None, None]
        * weight_z[None, None, :, None],
    }


def rate(field, second_value, left_data, right_data, tables):
    summed = terms_first(field, tables) + second_value + terms_third(field, tables)
    change = -summed
    face_weight = tables["face_weight"]
    change = change.at[0].add(face_weight * (left_data - robin_gain * field[0]))
    change = change.at[-1].add(face_weight * (right_data - robin_gain * field[-1]))
    return change / tables["lumped"]


def advance(opening, left_hist, right_hist, sections, second_terms, tables):
    step_len = step_size()
    opening_coef, coef_mu, coef_nu, coef_tilde = rkc_table(sections)
    left_trace = [opening[0]]
    right_trace = [opening[-1]]
    earlier = opening
    current = opening + opening_coef * step_len * rate(
        opening, second_terms(opening), left_hist[0], right_hist[0], tables
    )
    for section in range(2, SMAX + 1):
        updated = (
            coef_mu[section] * current
            + coef_nu[section] * earlier
            + coef_tilde[section]
            * step_len
            * rate(current, second_terms(current), left_hist[0], right_hist[0], tables)
        )
        active = section <= sections
        earlier, current = (
            jnp.where(active, current, earlier),
            jnp.where(active, updated, current),
        )
    return (current, jnp.stack(left_trace), jnp.stack(right_trace))


def local(initial_field, opening_guess, conductivity, capacity, section_count):
    sections = section_count[0]
    tables = build_tables(conductivity, capacity)
    kappa_follow = shifted_2(conductivity[:, :1], "gy", -1)
    kappa_y = along_second(jnp.concatenate([conductivity, kappa_follow], axis=1))

    def second_terms(field):
        following = shifted_2(field[:, :1], "gy", -1)
        interior, spill = terms_second(jnp.concatenate([field, following], axis=1), kappa_y, tables)
        arrived = shifted_2(spill, "gy", 1)
        return interior.at[:, 0].add(arrived)

    hist_shape = (STEPS,) + initial_field.shape[1:]
    left_hist = jnp.zeros(hist_shape, jnp.float32)
    right_hist = jnp.zeros(hist_shape, jnp.float32)
    first_block = lax.axis_index("ta") == 0
    opening = jnp.where(first_block, initial_field, opening_guess[0])
    finish = opening
    for sweep in range(ITERS):
        finish, left_trace, right_trace = advance(
            opening, left_hist, right_hist, sections, second_terms, tables
        )
        send_left = 2.0 * robin_gain * left_trace - left_hist
        send_right = 2.0 * robin_gain * right_trace - right_hist
        left_hist = shifted_3(send_right, "gx", 1)
        right_hist = shifted_3(send_left, "gx", -1)
        if sweep + 1 < ITERS:
            received = shifted_3(finish, "ta", 1)
            opening = jnp.where(first_block, initial_field, received)
    block_end = finish[None]
    robin_next = jnp.stack([left_hist, right_hist], axis=0)[None]
    return (block_end, robin_next)


def solution(mesh):
    return jax.shard_map(
        local,
        mesh=mesh,
        in_specs=(
            P("gx", "gy", None, None),
            P("ta", "gx", "gy", None, None),
            P("gx", "gy", None, None),
            P("gx", "gy", None, None),
            P("gx"),
        ),
        out_specs=(P("ta", "gx", "gy", None, None), P("gx", None, "ta", "gy", None, None)),
        check_vma=False,
    )
```

profile of v0, /device:TPU:0, one launch (start us, length us, event | category | flops | bytes accessed | tf_op | source)
XLA Modules:
  0.0 123.3 jit_solution(15214522284580454170)
XLA Ops:
  0.6 1.1 bitcast_select_fusion
  1.8 5.1 %collective-permute-start = (f32[11,1,5,128]{3,1,2,0:T(1,128)S(1)}, f32[11,1,5,128]{3,1,2,0:T(1,128)S(1)}, u32[]{:S(2)}, u32[]{:S(2)}) collective-permute-start(f32[11,1,5,128]{3,1,2,0:T(1,128)S(1)} %slice.1973), channel_id=1, source_target_pairs={{0,3},{1,0},{2,1},{3,2},{4,7},{5,4},{6,5},{7,6},{8,11},{9,8},{10,9... | collective-permute-start | bytes 84488 | tf_op jit(solution)/shard_map/ppermute | solution.py:25
  6.9 0.8 collective-permute-start.1
  8.8 0.6 copy-done.5
  10.6 0.8 slice-done.1
  11.5 0.8 slice-done
  12.4 0.6 copy-done.7
  15.9 1.3 %collective-permute-start.2 = (f32[11,5,128]{2,0,1:T(8,128)S(1)}, f32[11,5,128]{2,0,1:T(8,128)S(1)}, u32[]{:S(2)}, u32[]{:S(2)}) collective-permute-start(f32[11,5,128]{2,0,1:T(8,128)S(1)} %bitcast.933), channel_id=1, source_target_pairs={{0,1},{1,2},{2,3},{3,0},{4,5},{5,6},{6,7},{7,4},{8,9},{9,10},{10,1... | collective-permute-start | bytes 84488 | tf_op jit(solution)/shard_map/ppermute | solution.py:25
  19.0 2.7 %collective-permute-done.2 = f32[11,5,128]{2,0,1:T(8,128)S(1)} collective-permute-done((f32[11,5,128]{2,0,1:T(8,128)S(1)}, f32[11,5,128]{2,0,1:T(8,128)S(1)}, u32[]{:S(2)}, u32[]{:S(2)}) %collective-permute-start.2) | collective-permute-done | bytes 28192 | tf_op jit(solution)/shard_map/ppermute | solution.py:25
  22.1 0.7 copy-done.4
  23.2 0.9 copy-done.1
  26.1 2.8 %collective-permute-done.3 = f32[11,1,5,128]{3,1,2,0:T(1,128)S(1)} collective-permute-done((f32[11,1,5,128]{3,1,2,0:T(1,128)S(1)}, f32[11,1,5,128]{3,1,2,0:T(1,128)S(1)}, u32[]{:S(2)}, u32[]{:S(2)}) %collective-permute-start.3) | collective-permute-done | bytes 28192 | tf_op jit(solution)/shard_map/ppermute | solution.py:25
  30.2 5.7 %collective-permute-done.4 = f32[11,5,128]{2,0,1:T(8,128)S(1)} collective-permute-done((f32[11,5,128]{2,0,1:T(8,128)S(1)}, f32[11,5,128]{2,0,1:T(8,128)S(1)}, u32[]{:S(2)}, u32[]{:S(2)}) %collective-permute-start.4) | collective-permute-done | bytes 28192 | tf_op jit(solution)/shard_map/ppermute | solution.py:25
  38.7 2.8 %collective-permute-done.5 = f32[11,1,5,128]{3,1,2,0:T(1,128)S(1)} collective-permute-done((f32[11,1,5,128]{3,1,2,0:T(1,128)S(1)}, f32[11,1,5,128]{3,1,2,0:T(1,128)S(1)}, u32[]{:S(2)}, u32[]{:S(2)}) %collective-permute-start.5) | collective-permute-done | bytes 28192 | tf_op jit(solution)/shard_map/ppermute | solution.py:25
  42.9 5.5 %collective-permute-done.6 = f32[11,5,128]{2,0,1:T(8,128)S(1)} collective-permute-done((f32[11,5,128]{2,0,1:T(8,128)S(1)}, f32[11,5,128]{2,0,1:T(8,128)S(1)}, u32[]{:S(2)}, u32[]{:S(2)}) %collective-permute-start.6) | collective-permute-done | bytes 28192 | tf_op jit(solution)/shard_map/ppermute | solution.py:25
  51.4 2.8 %collective-permute-done.7 = f32[11,1,5,128]{3,1,2,0:T(1,128)S(1)} collective-permute-done((f32[11,1,5,128]{3,1,2,0:T(1,128)S(1)}, f32[11,1,5,128]{3,1,2,0:T(1,128)S(1)}, u32[]{:S(2)}, u32[]{:S(2)}) %collective-permute-start.7) | collective-permute-done | bytes 28192 | tf_op jit(solution)/shard_map/ppermute | solution.py:25
  55.6 5.5 %collective-permute-done.8 = f32[11,5,128]{2,0,1:T(8,128)S(1)} collective-permute-done((f32[11,5,128]{2,0,1:T(8,128)S(1)}, f32[11,5,128]{2,0,1:T(8,128)S(1)}, u32[]{:S(2)}, u32[]{:S(2)}) %collective-permute-start.8) | collective-permute-done | bytes 28192 | tf_op jit(solution)/shard_map/ppermute | solution.py:25
  61.7 1.3 %collective-permute-start.9 = (f32[11,5,5,128]{3,1,2,0:T(8,128)S(1)}, f32[11,5,5,128]{3,1,2,0:T(8,128)S(1)}, u32[]{:S(2)}, u32[]{:S(2)}) collective-permute-start(f32[11,5,5,128]{3,1,2,0:T(8,128)S(1)} %add_select_fusion.2), channel_id=1, source_target_pairs={{0,4},{4,8},{8,12},{1,5},{5,9},{9,13},{2,6},{6,10},{10,14},{3,7},{... | collective-permute-start | bytes 422408 | tf_op jit(solution)/shard_map/ppermute | solution.py:31
  63.0 1.3 %collective-permute-start.13 = (f32[1,5,5,128]{3,1,2,0:T(8,128)S(1)}, f32[1,5,5,128]{3,1,2,0:T(8,128)S(1)}, u32[]{:S(2)}, u32[]{:S(2)}) collective-permute-start(f32[1,5,5,128]{3,1,2,0:T(8,128)S(1)} %get-tuple-element.606), channel_id=1, source_target_pairs={{16,0},{17,1},{18,2},{19,3},{20,4},{21,5},{22,6},{23,7},{24,8},{25... | collective-permute-start | bytes 38408 | tf_op jit(solution)/shard_map/ppermute | solution.py:31
  64.3 4.5 %collective-permute-start.12 = (f32[1,5,5,128]{3,1,2,0:T(8,128)S(1)}, f32[1,5,5,128]{3,1,2,0:T(8,128)S(1)}, u32[]{:S(2)}, u32[]{:S(2)}) collective-permute-start(f32[1,5,5,128]{3,1,2,0:T(8,128)S(1)} %get-tuple-element.607), channel_id=1, source_target_pairs={{0,16},{1,17},{2,18},{3,19},{4,20},{5,21},{6,22},{7,23},{8,24},{9,... | collective-permute-start | bytes 38408 | tf_op jit(solution)/shard_map/ppermute | solution.py:31
  71.2 2.8 %collective-permute-done.10 = f32[11,1,5,128]{3,1,2,0:T(1,128)S(1)} collective-permute-done((f32[11,1,5,128]{3,1,2,0:T(1,128)S(1)}, f32[11,1,5,128]{3,1,2,0:T(1,128)S(1)}, u32[]{:S(2)}, u32[]{:S(2)}) %collective-permute-start.10) | collective-permute-done | bytes 28192 | tf_op jit(solution)/shard_map/ppermute | solution.py:25
  75.3 5.5 %collective-permute-done.11 = f32[11,5,128]{2,0,1:T(8,128)S(1)} collective-permute-done((f32[11,5,128]{2,0,1:T(8,128)S(1)}, f32[11,5,128]{2,0,1:T(8,128)S(1)}, u32[]{:S(2)}, u32[]{:S(2)}) %collective-permute-start.11) | collective-permute-done | bytes 28192 | tf_op jit(solution)/shard_map/ppermute | solution.py:25
  83.8 1.3 %collective-permute-start.21 = (f32[1,5,5,128]{3,1,2,0:T(8,128)S(1)}, f32[1,5,5,128]{3,1,2,0:T(8,128)S(1)}, u32[]{:S(2)}, u32[]{:S(2)}) collective-permute-start(f32[1,5,5,128]{3,1,2,0:T(8,128)S(1)} %get-tuple-element.590), channel_id=1, source_target_pairs={{16,0},{17,1},{18,2},{19,3},{20,4},{21,5},{22,6},{23,7},{24,8},{25... | collective-permute-start | bytes 38408 | tf_op jit(solution)/shard_map/ppermute | solution.py:31
  85.1 4.5 %collective-permute-start.20 = (f32[1,5,5,128]{3,1,2,0:T(8,128)S(1)}, f32[1,5,5,128]{3,1,2,0:T(8,128)S(1)}, u32[]{:S(2)}, u32[]{:S(2)}) collective-permute-start(f32[1,5,5,128]{3,1,2,0:T(8,128)S(1)} %get-tuple-element.588), channel_id=1, source_target_pairs={{0,16},{1,17},{2,18},{3,19},{4,20},{5,21},{6,22},{7,23},{8,24},{9,... | collective-permute-start | bytes 38408 | tf_op jit(solution)/shard_map/ppermute | solution.py:31
  90.8 1.8 %collective-permute-start.15 = (f32[11,5,128]{2,0,1:T(8,128)S(1)}, f32[11,5,128]{2,0,1:T(8,128)S(1)}, u32[]{:S(2)}, u32[]{:S(2)}) collective-permute-start(f32[11,5,128]{2,0,1:T(8,128)S(1)} %bitcast.934), channel_id=1, source_target_pairs={{0,1},{1,2},{2,3},{3,0},{4,5},{5,6},{6,7},{7,4},{8,9},{9,10},{10,1... | collective-permute-start | bytes 84488 | tf_op jit(solution)/shard_map/ppermute | solution.py:25
  92.6 0.6 copy.763
  93.5 3.2 %collective-permute-done.15 = f32[11,5,128]{2,0,1:T(8,128)S(1)} collective-permute-done((f32[11,5,128]{2,0,1:T(8,128)S(1)}, f32[11,5,128]{2,0,1:T(8,128)S(1)}, u32[]{:S(2)}, u32[]{:S(2)}) %collective-permute-start.15) | collective-permute-done | bytes 28192 | tf_op jit(solution)/shard_map/ppermute | solution.py:25
  99.7 2.8 %collective-permute-done.16 = f32[11,1,5,128]{3,1,2,0:T(1,128)S(1)} collective-permute-done((f32[11,1,5,128]{3,1,2,0:T(1,128)S(1)}, f32[11,1,5,128]{3,1,2,0:T(1,128)S(1)}, u32[]{:S(2)}, u32[]{:S(2)}) %collective-permute-start.16) | collective-permute-done | bytes 28192 | tf_op jit(solution)/shard_map/ppermute | solution.py:25
  103.8 5.5 %collective-permute-done.17 = f32[11,5,128]{2,0,1:T(8,128)S(1)} collective-permute-done((f32[11,5,128]{2,0,1:T(8,128)S(1)}, f32[11,5,128]{2,0,1:T(8,128)S(1)}, u32[]{:S(2)}, u32[]{:S(2)}) %collective-permute-start.17) | collective-permute-done | bytes 28192 | tf_op jit(solution)/shard_map/ppermute | solution.py:25
  112.3 2.8 %collective-permute-done.18 = f32[11,1,5,128]{3,1,2,0:T(1,128)S(1)} collective-permute-done((f32[11,1,5,128]{3,1,2,0:T(1,128)S(1)}, f32[11,1,5,128]{3,1,2,0:T(1,128)S(1)}, u32[]{:S(2)}, u32[]{:S(2)}) %collective-permute-start.18) | collective-permute-done | bytes 28192 | tf_op jit(solution)/shard_map/ppermute | solution.py:25
  116.4 5.5 %collective-permute-done.19 = f32[11,5,128]{2,0,1:T(8,128)S(1)} collective-permute-done((f32[11,5,128]{2,0,1:T(8,128)S(1)}, f32[11,5,128]{2,0,1:T(8,128)S(1)}, u32[]{:S(2)}, u32[]{:S(2)}) %collective-permute-start.19) | collective-permute-done | bytes 28192 | tf_op jit(solution)/shard_map/ppermute | solution.py:25
  122.5 0.8 copy.762
  (360 shorter events, 34.0 us)
Async XLA Ops:
  1.7 8.6 %copy-start.2 = (f32[11,5,5,128]{3,1,2,0:T(8,128)}, f32[11,5,5,128]{3,1,2,0:T(8,128)S(1)}, u32[]{:S(2)}) copy-start(f32[11,5,5,128]{3,1,2,0:T(8,128)S(1)} %bitcast_select_fusion) | copy-start | bytes 422404
  1.8 5.1 %slice-start.2 = ((f32[11,5,5,128]{3,0,2,1:T(8,128)}), f32[11,1,5,128]{3,0,2,1:T(8,128)S(1)}, s32[]{:S(2)}) async-start(f32[11,5,5,128]{3,0,2,1:T(8,128)} %param.108), calls=%async_computation.2 | async-start | bytes 81920 | tf_op jit(solution)/shard_map/slice | solution.py:225
  1.8 6.0 %copy-start.6 = (f32[11,5,5,128]{3,0,2,1:T(8,128)S(1)}, f32[11,5,5,128]{3,0,2,1:T(8,128)}, u32[]{:S(2)}) copy-start(f32[11,5,5,128]{3,0,2,1:T(8,128)} %param.108) | copy-start | bytes 422404
  1.8 12.7 %collective-permute-start = (f32[11,1,5,128]{3,1,2,0:T(1,128)S(1)}, f32[11,1,5,128]{3,1,2,0:T(1,128)S(1)}, u32[]{:S(2)}, u32[]{:S(2)}) collective-permute-start(f32[11,1,5,128]{3,1,2,0:T(1,128)S(1)} %slice.1973), channel_id=1, source_target_pairs={{0,3},{1,0},{2,1},{3,2},{4,7},{5,4},{6,5},{7,6},{8,11},{9,8},{10,9... | collective-permute-start | bytes 84488 | tf_op jit(solution)/shard_map/ppermute | solution.py:25
  6.9 7.6 %collective-permute-start.1 = (f32[11,1,5,128]{3,1,2,0:T(1,128)S(1)}, f32[11,1,5,128]{3,1,2,0:T(1,128)S(1)}, u32[]{:S(2)}, u32[]{:S(2)}) collective-permute-start(f32[11,1,5,128]{3,1,2,0:T(1,128)S(1)} %copy.983), channel_id=1, source_target_pairs={{0,3},{1,0},{2,1},{3,2},{4,7},{5,4},{6,5},{7,6},{8,11},{9,8},{10,9... | collective-permute-start | bytes 84488 | tf_op jit(solution)/shard_map/ppermute | solution.py:25
  7.9 2.6 %copy-start = (f32[11,5,5,128]{3,2,1,0:T(8,128)}, f32[11,5,5,128]{3,2,1,0:T(8,128)S(1)}, u32[]{:S(2)}) copy-start(f32[11,5,5,128]{3,2,1,0:T(8,128)S(1)} %copy.600) | copy-start | bytes 422404
  13.9 0.9 copy-start.3
  15.9 1.4 %slice-start.3 = ((f32[2,6,5,5,128]{4,1,3,2,0:T(8,128)}), f32[2,1,5,5,128]{4,1,3,2,0:T(1,128)S(1)}, s32[]{:S(2)}) async-start(f32[2,6,5,5,128]{4,1,3,2,0:T(8,128)} %copy-done.8), calls=%async_computation.3 | async-start | bytes 51200 | tf_op jit(solution)/shard_map/slice.1400
  15.9 2.5 %copy-start.9 = (f32[2,6,5,5,128]{4,1,3,2,0:T(8,128)S(1)}, f32[2,6,5,5,128]{4,1,3,2,0:T(8,128)}, u32[]{:S(2)}) copy-start(f32[2,6,5,5,128]{4,1,3,2,0:T(8,128)} %copy-done.8) | copy-start | bytes 460804
  15.9 5.9 %collective-permute-start.2 = (f32[11,5,128]{2,0,1:T(8,128)S(1)}, f32[11,5,128]{2,0,1:T(8,128)S(1)}, u32[]{:S(2)}, u32[]{:S(2)}) collective-permute-start(f32[11,5,128]{2,0,1:T(8,128)S(1)} %bitcast.933), channel_id=1, source_target_pairs={{0,1},{1,2},{2,3},{3,0},{4,5},{5,6},{6,7},{7,4},{8,9},{9,10},{10,1... | collective-permute-start | bytes 84488 | tf_op jit(solution)/shard_map/ppermute | solution.py:25
  21.9 0.9 copy-start.4
  23.1 0.9 copy-start.1
  25.0 3.9 %collective-permute-start.3 = (f32[11,1,5,128]{3,1,2,0:T(1,128)S(1)}, f32[11,1,5,128]{3,1,2,0:T(1,128)S(1)}, u32[]{:S(2)}, u32[]{:S(2)}) collective-permute-start(f32[11,1,5,128]{3,1,2,0:T(1,128)S(1)} %slice.1995), channel_id=1, source_target_pairs={{0,3},{1,0},{2,1},{3,2},{4,7},{5,4},{6,5},{7,6},{8,11},{9,8},{10,9... | collective-permute-start | bytes 84488 | tf_op jit(solution)/shard_map/ppermute | solution.py:25
  29.9 6.0 %collective-permute-start.4 = (f32[11,5,128]{2,0,1:T(8,128)S(1)}, f32[11,5,128]{2,0,1:T(8,128)S(1)}, u32[]{:S(2)}, u32[]{:S(2)}) collective-permute-start(f32[11,5,128]{2,0,1:T(8,128)S(1)} %bitcast.935), channel_id=1, source_target_pairs={{0,1},{1,2},{2,3},{3,0},{4,5},{5,6},{6,7},{7,4},{8,9},{9,10},{10,1... | collective-permute-start | bytes 84488 | tf_op jit(solution)/shard_map/ppermute | solution.py:25
  37.7 3.9 %collective-permute-start.5 = (f32[11,1,5,128]{3,1,2,0:T(1,128)S(1)}, f32[11,1,5,128]{3,1,2,0:T(1,128)S(1)}, u32[]{:S(2)}, u32[]{:S(2)}) collective-permute-start(f32[11,1,5,128]{3,1,2,0:T(1,128)S(1)} %slice.2014), channel_id=1, source_target_pairs={{0,3},{1,0},{2,1},{3,2},{4,7},{5,4},{6,5},{7,6},{8,11},{9,8},{10,9... | collective-permute-start | bytes 84488 | tf_op jit(solution)/shard_map/ppermute | solution.py:25
  42.6 5.9 %collective-permute-start.6 = (f32[11,5,128]{2,0,1:T(8,128)S(1)}, f32[11,5,128]{2,0,1:T(8,128)S(1)}, u32[]{:S(2)}, u32[]{:S(2)}) collective-permute-start(f32[11,5,128]{2,0,1:T(8,128)S(1)} %bitcast.936), channel_id=1, source_target_pairs={{0,1},{1,2},{2,3},{3,0},{4,5},{5,6},{6,7},{7,4},{8,9},{9,10},{10,1... | collective-permute-start | bytes 84488 | tf_op jit(solution)/shard_map/ppermute | solution.py:25
  50.4 3.9 %collective-permute-start.7 = (f32[11,1,5,128]{3,1,2,0:T(1,128)S(1)}, f32[11,1,5,128]{3,1,2,0:T(1,128)S(1)}, u32[]{:S(2)}, u32[]{:S(2)}) collective-permute-start(f32[11,1,5,128]{3,1,2,0:T(1,128)S(1)} %slice.2033), channel_id=1, source_target_pairs={{0,3},{1,0},{2,1},{3,2},{4,7},{5,4},{6,5},{7,6},{8,11},{9,8},{10,9... | collective-permute-start | bytes 84488 | tf_op jit(solution)/shard_map/ppermute | solution.py:25
  55.3 5.9 %collective-permute-start.8 = (f32[11,5,128]{2,0,1:T(8,128)S(1)}, f32[11,5,128]{2,0,1:T(8,128)S(1)}, u32[]{:S(2)}, u32[]{:S(2)}) collective-permute-start(f32[11,5,128]{2,0,1:T(8,128)S(1)} %bitcast.937), channel_id=1, source_target_pairs={{0,1},{1,2},{2,3},{3,0},{4,5},{5,6},{6,7},{7,4},{8,9},{9,10},{10,1... | collective-permute-start | bytes 84488 | tf_op jit(solution)/shard_map/ppermute | solution.py:25
  61.5 7.4 %copy-start.10 = (f32[11,5,5,128]{3,0,2,1:T(8,128)S(1)}, f32[11,5,5,128]{3,0,2,1:T(8,128)}, u32[]{:S(2)}) copy-start(f32[11,5,5,128]{3,0,2,1:T(8,128)} %param.106) | copy-start | bytes 422404
  61.7 7.2 %collective-permute-start.9 = (f32[11,5,5,128]{3,1,2,0:T(8,128)S(1)}, f32[11,5,5,128]{3,1,2,0:T(8,128)S(1)}, u32[]{:S(2)}, u32[]{:S(2)}) collective-permute-start(f32[11,5,5,128]{3,1,2,0:T(8,128)S(1)} %add_select_fusion.2), channel_id=1, source_target_pairs={{0,4},{4,8},{8,12},{1,5},{5,9},{9,13},{2,6},{6,10},{10,14},{3,7},{... | collective-permute-start | bytes 422408 | tf_op jit(solution)/shard_map/ppermute | solution.py:31
  63.0 18.2 %collective-permute-start.13 = (f32[1,5,5,128]{3,1,2,0:T(8,128)S(1)}, f32[1,5,5,128]{3,1,2,0:T(8,128)S(1)}, u32[]{:S(2)}, u32[]{:S(2)}) collective-permute-start(f32[1,5,5,128]{3,1,2,0:T(8,128)S(1)} %get-tuple-element.606), channel_id=1, source_target_pairs={{16,0},{17,1},{18,2},{19,3},{20,4},{21,5},{22,6},{23,7},{24,8},{25... | collective-permute-start | bytes 38408 | tf_op jit(solution)/shard_map/ppermute | solution.py:31
  64.3 16.8 %collective-permute-start.12 = (f32[1,5,5,128]{3,1,2,0:T(8,128)S(1)}, f32[1,5,5,128]{3,1,2,0:T(8,128)S(1)}, u32[]{:S(2)}, u32[]{:S(2)}) collective-permute-start(f32[1,5,5,128]{3,1,2,0:T(8,128)S(1)} %get-tuple-element.607), channel_id=1, source_target_pairs={{0,16},{1,17},{2,18},{3,19},{4,20},{5,21},{6,22},{7,23},{8,24},{9,... | collective-permute-start | bytes 38408 | tf_op jit(solution)/shard_map/ppermute | solution.py:31
  70.2 3.9 %collective-permute-start.10 = (f32[11,1,5,128]{3,1,2,0:T(1,128)S(1)}, f32[11,1,5,128]{3,1,2,0:T(1,128)S(1)}, u32[]{:S(2)}, u32[]{:S(2)}) collective-permute-start(f32[11,1,5,128]{3,1,2,0:T(1,128)S(1)} %slice.2052), channel_id=1, source_target_pairs={{0,3},{1,0},{2,1},{3,2},{4,7},{5,4},{6,5},{7,6},{8,11},{9,8},{10,9... | collective-permute-start | bytes 84488 | tf_op jit(solution)/shard_map/ppermute | solution.py:25
  75.0 5.9 %collective-permute-start.11 = (f32[11,5,128]{2,0,1:T(8,128)S(1)}, f32[11,5,128]{2,0,1:T(8,128)S(1)}, u32[]{:S(2)}, u32[]{:S(2)}) collective-permute-start(f32[11,5,128]{2,0,1:T(8,128)S(1)} %bitcast.938), channel_id=1, source_target_pairs={{0,1},{1,2},{2,3},{3,0},{4,5},{5,6},{6,7},{7,4},{8,9},{9,10},{10,1... | collective-permute-start | bytes 84488 | tf_op jit(solution)/shard_map/ppermute | solution.py:25
  83.5 6.2 %collective-permute-start.14 = (f32[11,1,5,128]{3,1,2,0:T(1,128)S(1)}, f32[11,1,5,128]{3,1,2,0:T(1,128)S(1)}, u32[]{:S(2)}, u32[]{:S(2)}) collective-permute-start(f32[11,1,5,128]{3,1,2,0:T(1,128)S(1)} %slice.2071), channel_id=1, source_target_pairs={{0,3},{1,0},{2,1},{3,2},{4,7},{5,4},{6,5},{7,6},{8,11},{9,8},{10,9... | collective-permute-start | bytes 84488 | tf_op jit(solution)/shard_map/ppermute | solution.py:25
  83.8 8.8 %collective-permute-start.21 = (f32[1,5,5,128]{3,1,2,0:T(8,128)S(1)}, f32[1,5,5,128]{3,1,2,0:T(8,128)S(1)}, u32[]{:S(2)}, u32[]{:S(2)}) collective-permute-start(f32[1,5,5,128]{3,1,2,0:T(8,128)S(1)} %get-tuple-element.590), channel_id=1, source_target_pairs={{16,0},{17,1},{18,2},{19,3},{20,4},{21,5},{22,6},{23,7},{24,8},{25... | collective-permute-start | bytes 38408 | tf_op jit(solution)/shard_map/ppermute | solution.py:31
  85.1 7.5 %collective-permute-start.20 = (f32[1,5,5,128]{3,1,2,0:T(8,128)S(1)}, f32[1,5,5,128]{3,1,2,0:T(8,128)S(1)}, u32[]{:S(2)}, u32[]{:S(2)}) collective-permute-start(f32[1,5,5,128]{3,1,2,0:T(8,128)S(1)} %get-tuple-element.588), channel_id=1, source_target_pairs={{0,16},{1,17},{2,18},{3,19},{4,20},{5,21},{6,22},{7,23},{8,24},{9,... | collective-permute-start | bytes 38408 | tf_op jit(solution)/shard_map/ppermute | solution.py:31
  90.8 5.9 %collective-permute-start.15 = (f32[11,5,128]{2,0,1:T(8,128)S(1)}, f32[11,5,128]{2,0,1:T(8,128)S(1)}, u32[]{:S(2)}, u32[]{:S(2)}) collective-permute-start(f32[11,5,128]{2,0,1:T(8,128)S(1)} %bitcast.934), channel_id=1, source_target_pairs={{0,1},{1,2},{2,3},{3,0},{4,5},{5,6},{6,7},{7,4},{8,9},{9,10},{10,1... | collective-permute-start | bytes 84488 | tf_op jit(solution)/shard_map/ppermute | solution.py:25
  98.4 4.1 %collective-permute-start.16 = (f32[11,1,5,128]{3,1,2,0:T(1,128)S(1)}, f32[11,1,5,128]{3,1,2,0:T(1,128)S(1)}, u32[]{:S(2)}, u32[]{:S(2)}) collective-permute-start(f32[11,1,5,128]{3,1,2,0:T(1,128)S(1)} %slice.2090), channel_id=1, source_target_pairs={{0,3},{1,0},{2,1},{3,2},{4,7},{5,4},{6,5},{7,6},{8,11},{9,8},{10,9... | collective-permute-start | bytes 84488 | tf_op jit(solution)/shard_map/ppermute | solution.py:25
  103.5 5.9 %collective-permute-start.17 = (f32[11,5,128]{2,0,1:T(8,128)S(1)}, f32[11,5,128]{2,0,1:T(8,128)S(1)}, u32[]{:S(2)}, u32[]{:S(2)}) collective-permute-start(f32[11,5,128]{2,0,1:T(8,128)S(1)} %bitcast.939), channel_id=1, source_target_pairs={{0,1},{1,2},{2,3},{3,0},{4,5},{5,6},{6,7},{7,4},{8,9},{9,10},{10,1... | collective-permute-start | bytes 84488 | tf_op jit(solution)/shard_map/ppermute | solution.py:25
  111.2 3.9 %collective-permute-start.18 = (f32[11,1,5,128]{3,1,2,0:T(1,128)S(1)}, f32[11,1,5,128]{3,1,2,0:T(1,128)S(1)}, u32[]{:S(2)}, u32[]{:S(2)}) collective-permute-start(f32[11,1,5,128]{3,1,2,0:T(1,128)S(1)} %slice.2109), channel_id=1, source_target_pairs={{0,3},{1,0},{2,1},{3,2},{4,7},{5,4},{6,5},{7,6},{8,11},{9,8},{10,9... | collective-permute-start | bytes 84488 | tf_op jit(solution)/shard_map/ppermute | solution.py:25
  116.0 5.9 %collective-permute-start.19 = (f32[11,5,128]{2,0,1:T(8,128)S(1)}, f32[11,5,128]{2,0,1:T(8,128)S(1)}, u32[]{:S(2)}, u32[]{:S(2)}) collective-permute-start(f32[11,5,128]{2,0,1:T(8,128)S(1)} %bitcast.940), channel_id=1, source_target_pairs={{0,1},{1,2},{2,3},{3,0},{4,5},{5,6},{6,7},{7,4},{8,9},{9,10},{10,1... | collective-permute-start | bytes 84488 | tf_op jit(solution)/shard_map/ppermute | solution.py:25
  (8 other events, 5.9 us)
where the time goes:
time: 124 us; the launch traced here: 123 us
  waiting for transfers between devices  56.3 us (45%)
  starting transfers between devices  23 us (19%)
  matrix products  17.9 us (14%)
  local copies, waits for them, and re-layouts  16.3 us (13%)
  other arithmetic  5.8 us (5%)
  between operations  3.97 us (3%)
    ppermute x17, waiting for transfers between devices, shifted_2(): return lax.ppermute(value, axis, pairs)  56.3 us
    ppermute x5, starting transfers between devices, shifted_3(): lax.ppermute(value, axis, [(source, source + steps) for source in range(l...  13 us
    ppermute x17, starting transfers between devices, shifted_2(): return lax.ppermute(value, axis, pairs)  10 us
    unnamed x33, local copies, waits for them, and re-layouts  5.87 us
    dot_general x8, matrix products, terms_third(): returned = jnp.einsum('ab,xyae->xybe', derivative, flux, precision=highest)  3.1 us
    dot_general x8, matrix products, terms_second(): jnp.einsum('ab,xea...->xeb...', derivative, flux, precision=highest)  3.08 us
    dot_general x8, matrix products, terms_third(): slopes = jnp.einsum('ab,xybe->xyae', derivative, element, precision=highest)  3.05 us
    dot_general x8, matrix products, terms_first(): jnp.einsum('ab,ea...->eb...', derivative, flux, precision=highest)  2.93 us
  transfers between devices with their start and end apart: 22, of which 14 were waited for; matrix products, arithmetic and copies ran while one was open for 12% of the time, Pallas kernels for 0%

commit v1 on v0

v1 whole, which is shorter than its diff:
```python
import functools
import math

import jax
import jax.numpy as jnp
import ml_dtypes
import numpy as np
from jax import lax
from jax.experimental import pallas as pl
from jax.experimental.pallas import tpu as pltpu
from jax.sharding import PartitionSpec as P

ITERS = 2
SMIN = 3
SMAX = 4
LANES = 128
PLANES = 6
MESH = pl.DeviceIdType.MESH

robin_gain = 2.0
kappa_top = 2.0
capacity_low = 0.5
damping = 0.05


def gll_tables():
    root_seven = math.sqrt(7.0)
    outer = math.sqrt(1.0 / 3.0 + 2.0 * root_seven / 21.0)
    closer = math.sqrt(1.0 / 3.0 - 2.0 * root_seven / 21.0)
    points = np.array([-1.0, -outer, -closer, closer, outer, 1.0])
    low, high = (14.0 - root_seven) / 30.0, (14.0 + root_seven) / 30.0
    weights = np.array([1.0 / 15.0, low, high, high, low, 1.0 / 15.0])
    products = np.array(
        [np.prod([points[i] - points[k] for k in range(6) if k != i]) for i in range(6)]
    )
    derivative = np.zeros((6, 6))
    for i in range(6):
        for k in range(6):
            if i != k:
                derivative[i, k] = products[i] / (products[k] * (points[i] - points[k]))
    for i in range(6):
        derivative[i, i] = -derivative[i].sum()
    return (points, weights, derivative)


def line_weights(count, closed):
    weights = gll_tables()[1]
    pattern = np.array([weights[i % 5] if i % 5 else 2.0 * weights[0] for i in range(count)])
    if closed:
        pattern[0] = weights[0]
        pattern[-1] = weights[0]
    return pattern


def step_size():
    points, weights, derivative = gll_tables()
    row_sums = np.abs(derivative).sum(axis=1)
    gersh_bound = max(
        float(np.sum(np.abs(derivative[:, i]) * weights * row_sums) / weights[i]) for i in range(6)
    )
    spectral = kappa_top / capacity_low * 3.0 * gersh_bound + robin_gain / (
        capacity_low * weights[0]
    )
    return float(0.8 * 1.93 * SMIN**2 / spectral)


def rkc_table(sections):
    shifted = 1.0 + damping / sections**2
    cheb, derivs = [1.0, shifted], [0.0, 1.0]
    for j in range(2, SMAX + 1):
        cheb.append(2.0 * shifted * cheb[-1] - cheb[-2])
        derivs.append(2.0 * cheb[j - 1] + 2.0 * shifted * derivs[j - 1] - derivs[j - 2])
    spread = cheb[sections] / derivs[sections]
    rows = [(1.0, 0.0, spread / shifted)]
    for j in range(2, SMAX + 1):
        if j <= sections:
            rows.append(
                (
                    2.0 * shifted * cheb[j - 1] / cheb[j],
                    -cheb[j - 2] / cheb[j],
                    2.0 * spread * cheb[j - 1] / cheb[j],
                )
            )
        else:
            rows.append((1.0, 0.0, 0.0))
    return np.array(rows)


def stacked(matrix):
    matrix = matrix.astype(np.float32)
    high = matrix.astype(ml_dtypes.bfloat16)
    low = (matrix - high.astype(np.float32)).astype(ml_dtypes.bfloat16)
    return np.concatenate([high, high, low], axis=1)


def row_order(px):
    inner = list(range(1, px - 1))
    first, second, third = inner[:3], inner[3:6], inner[6:]
    rows = [(0, q) for q in range(5)] + [(x, 0) for x in first]
    rows += [(px - 1, q) for q in range(5)] + [(x, 0) for x in second]
    rows += [(x, 0) for x in third]
    rows += [(x, q) for x in inner for q in range(1, 5)]
    while len(rows) % 8:
        rows.append((1, 1))
    return rows


LEAD = 24


def constants(px):
    points, quad, deriv = gll_tables()
    wx, wz = line_weights(px, True), line_weights(5, False)
    rows = row_order(px)
    count = len(rows)
    place = {}
    for r, node in enumerate(rows):
        place.setdefault(node, r)
    elements = (px - 1) // 5
    slope_rows = elements * 30 + px * 6
    padded = -(-slope_rows // 16) * 16
    slope = np.zeros((padded, count + LEAD))
    spread = np.zeros((padded, count + LEAD))
    r = 0
    for e in range(elements):
        for a in range(6):
            for q in range(5):
                for b in range(6):
                    slope[r, place[5 * e + b, q]] = deriv[a, b]
                spread[r, place[5 * e + a, q]] = quad[a] * wz[q]
                r += 1
    for x in range(px):
        for a in range(6):
            for b in range(5):
                slope[r, place[x, b]] = deriv[a, b]
            slope[r, count + place[x, 0]] = deriv[a, 5]
            source = place[x, a] if a < 5 else count + place[x, 0]
            spread[r, source] = quad[a] * wx[x]
            r += 1
    gather = np.zeros((count, px * 8), np.float32)
    scatter = np.zeros((px * 8, count), np.float32)
    for r, (x, q) in enumerate(rows):
        gather[r, 8 * x + q] = 1.0
    for (x, q), r in place.items():
        scatter[8 * x + q, r] = 1.0
    ones = np.ones((1, LANES))
    weight = np.array([wx[x] * wz[q] for x, q in rows])[:, None] * ones
    face = np.zeros((16, 1))
    face[0:5, 0] = wz
    face[8:13, 0] = wz
    table = np.stack([rkc_table(s).reshape(-1) for s in range(SMIN, SMAX + 1)])
    f32 = np.float32
    return (
        stacked(slope),
        stacked(slope.T),
        stacked(spread),
        gather,
        scatter,
        weight.astype(f32),
        (face * ones).astype(f32),
        table.astype(f32),
    )


def halves(value):
    high = value.astype(jnp.bfloat16)
    low = (value - high.astype(jnp.float32)).astype(jnp.bfloat16)
    return jnp.concatenate([high, low, high], axis=0)


def product(matrix, value):
    return jnp.dot(matrix, halves(value), preferred_element_type=jnp.float32)


def exact(matrix, value):
    return jnp.dot(
        matrix, value, preferred_element_type=jnp.float32, precision=lax.Precision.HIGHEST
    )


def plane(b):
    return slice(LANES * b, LANES * (b + 1))


def rolled(value, shift):
    parts = value.shape[1] // LANES
    return jnp.concatenate(
        [pltpu.roll(value[:, plane(b)], shift % LANES, 1) for b in range(parts)], axis=1
    )


def extended(value):
    return jnp.concatenate([value, rolled(value[:LEAD], -1)], axis=0)


def padded_rows(value):
    zeros = jnp.zeros((value.shape[0], 3, LANES), value.dtype)
    return jnp.concatenate([value, zeros], axis=1).reshape(8 * value.shape[0], LANES)


def kernel(
    sizes,
    step_len,
    init_ref, guess_ref, cond_ref, cap_ref, sec_ref,
    slope_ref, back_ref, spread_ref, gather_ref, scatter_ref, weight_ref, face_ref, table_ref,
    end_ref, robin_ref,
    field, opened, arrived, inv, flux_x, flux_y, part, raw_open, raw_in,
    send_y, recv_y, faces_in, faces_out, faces_next, hist, drive,
    raw_send, raw_recv, y_send, y_recv, f_send, f_recv, t_send, t_recv,
):
    n_gx, n_ta, n_gy = sizes
    quad, deriv = gll_tables()[1:]
    deriv = [[float(v) for v in row] for row in deriv]
    wy = [float(2.0 * quad[0])] + [float(quad[b]) for b in range(1, 5)] + [float(2.0 * quad[0])]
    gx, ta, gy = lax.axis_index("gx"), lax.axis_index("ta"), lax.axis_index("gy")
    ahead, behind = lax.rem(gy + 1, n_gy), lax.rem(gy + n_gy - 1, n_gy)
    has_left, has_right = gx > 0, gx < n_gx - 1
    has_before, has_after = ta > 0, ta < n_ta - 1

    barrier = pltpu.get_barrier_semaphore()

    def greet(target):
        pl.semaphore_signal(barrier, inc=1, device_id=target, device_id_type=MESH)

    greet({"gy": ahead})
    greet({"gy": behind})
    for there, name, index in (
        (has_left, "gx", gx - 1),
        (has_right, "gx", gx + 1),
        (has_before, "ta", ta - 1),
        (has_after, "ta", ta + 1),
    ):
        pl.when(there)(functools.partial(greet, {name: index}))

    first = ta == 0
    px = init_ref.shape[0]
    raw_open[...] = jnp.where(first, init_ref[:, 0], guess_ref[0, :, 0])
    expected = 2
    for there in (has_left, has_right, has_before, has_after):
        expected = expected + there.astype(jnp.int32)
    pl.semaphore_wait(barrier, expected)

    raws = []
    for k, source in enumerate((raw_open, cond_ref.at[:, 0], cap_ref.at[:, 0])):
        copy = pltpu.make_async_remote_copy(
            src_ref=source, dst_ref=raw_in.at[k], send_sem=raw_send.at[k],
            recv_sem=raw_recv.at[k], device_id={"gy": behind}, device_id_type=MESH,
        )
        copy.start()
        raws.append(copy)

    gather = gather_ref[...]
    weight = weight_ref[...]

    def packed(ref):
        wide = jnp.concatenate([padded_rows(ref[:, b]) for b in range(5)], axis=1)
        return exact(gather, wide)

    def set_tables(first_plane, count, kappa, capacity):
        spread_out = product(spread_ref[...], extended(kappa))
        for i in range(count):
            b = first_plane + i
            flux_x[:, plane(b)] = spread_out[:, plane(i)] * wy[b]
            flux_y[:, plane(b)] = kappa[:, plane(i)] * weight * float(quad[b])
            inv[:, plane(b)] = (step_len / wy[b]) / (capacity[:, plane(i)] * weight)

    own = slice(0, 5 * LANES)
    wide = jnp.concatenate(
        [
            padded_rows(jnp.where(first, init_ref[:, b], guess_ref[0, :, b]))
            for b in range(5)
        ],
        axis=1,
    )
    opened[:, own] = exact(gather, wide)
    set_tables(0, 5, packed(cond_ref), packed(cap_ref))
    for copy in raws:
        copy.wait()
    last = [exact(gather, padded_rows(raw_in[k])) for k in range(3)]
    opened[:, plane(5)] = last[0]
    set_tables(5, 1, last[1], last[2])

    field[0] = opened[...]
    field[1] = opened[...]
    faces_out[0] = opened[0:8]
    faces_out[1] = opened[8:16]
    drive[...] = jnp.zeros_like(drive)

    def face_copies(source, target, base):
        to_left = pltpu.make_async_remote_copy(
            src_ref=source.at[0], dst_ref=target.at[1], send_sem=f_send.at[base],
            recv_sem=f_recv.at[base + 1], device_id={"gx": gx - 1}, device_id_type=MESH,
        )
        to_right = pltpu.make_async_remote_copy(
            src_ref=source.at[1], dst_ref=target.at[0], send_sem=f_send.at[base + 1],
            recv_sem=f_recv.at[base], device_id={"gx": gx + 1}, device_id_type=MESH,
        )
        return to_left, to_right

    def start_faces(copies):
        pl.when(has_left)(copies[0].start)
        pl.when(has_right)(copies[1].start)

    def wait_faces(copies):
        @pl.when(has_left)
        def _():
            copies[0].wait_send()
            copies[1].wait_recv()

        @pl.when(has_right)
        def _():
            copies[1].wait_send()
            copies[0].wait_recv()

    faces = face_copies(faces_out, faces_in, 0)
    start_faces(faces)

    sections = sec_ref[0]
    face = face_ref[...]

    def coefficient(j, k):
        value = table_ref[0, 3 * j + k]
        for s in range(1, SMAX - SMIN + 1):
            value = jnp.where(sections == SMIN + s, table_ref[s, 3 * j + k], value)
        return value

    def combine(terms):
        total = terms[0]
        for term in terms[1:]:
            total = total + term
        return total

    def stage(sweep, j, carry):
        n = sweep * SMAX + j
        now = lax.rem(j, 2)
        later = 1 - now
        mu, nu, tilde = (coefficient(j, k) for k in range(3))
        u = [field[now, :, plane(b)] for b in range(PLANES)]
        flux = [
            flux_y[:, plane(a)] * combine([deriv[a][b] * u[b] for b in range(PLANES)])
            for a in range(PLANES)
        ]

        def returned(b):
            return combine([deriv[a][b] * flux[a] for a in range(PLANES)])

        edge = (returned(0), returned(5))
        copies = []
        for side, target in ((0, behind), (1, ahead)):
            send_y[n, side] = edge[side]
            copy = pltpu.make_async_remote_copy(
                src_ref=send_y.at[n, side], dst_ref=recv_y.at[n, 1 - side],
                send_sem=y_send.at[n, side], recv_sem=y_recv.at[n, 1 - side],
                device_id={"gy": target}, device_id_type=MESH,
            )
            copy.start()
            copies.append(copy)

        whole = field[now]
        slopes = product(slope_ref[...], extended(whole))
        back = product(back_ref[...], slopes * flux_x[...])
        count = whole.shape[0]
        wrapped = rolled(back[count:], 1)

        def assembled(b, second):
            value = back[:count, plane(b)] + second
            lead = value[:LEAD] + wrapped[:, plane(b)]
            top = lead[:16] + face * (robin_gain * wy[b]) * u[b][:16] - drive[:, plane(b)]
            return jnp.concatenate([top, lead[16:], value[LEAD:]], axis=0)

        for b in range(1, 5):
            total = assembled(b, returned(b))
            field[later, :, plane(b)] = (
                mu * u[b] + nu * field[later, :, plane(b)] - tilde * (inv[:, plane(b)] * total)
            )
        for side, b in ((0, 0), (1, 5)):
            total = assembled(b, edge[side])
            part[side] = (
                mu * u[b] + nu * field[later, :, plane(b)] - tilde * (inv[:, plane(b)] * total)
            )
        copies[0].wait()
        copies[1].wait()
        for side, b in ((0, 0), (1, 5)):
            field[later, :, plane(b)] = part[side] - tilde * (inv[:, plane(b)] * recv_y[n, side])
        return carry

    lax.fori_loop(0, SMAX, functools.partial(stage, 0), 0)

    onward = pltpu.make_async_remote_copy(
        src_ref=field.at[SMAX % 2], dst_ref=arrived, send_sem=t_send, recv_sem=t_recv,
        device_id={"ta": ta + 1}, device_id_type=MESH,
    )
    pl.when(has_after)(onward.start)

    wait_faces(faces)
    for side, there in ((0, has_left), (1, has_right)):
        @pl.when(there)
        def _():
            hist[side] = (2.0 * robin_gain) * faces_in[side]

        @pl.when(jnp.logical_not(there))
        def _():
            hist[side] = jnp.zeros(hist.shape[1:], jnp.float32)
    for b in range(PLANES):
        for side in range(2):
            rows = slice(8 * side, 8 * side + 8)
            drive[rows, plane(b)] = face[rows] * wy[b] * hist[side, :, plane(b)]

    pl.when(has_after)(onward.wait_send)

    @pl.when(has_before)
    def _():
        onward.wait_recv()
        field[0] = arrived[...]
        field[1] = arrived[...]

    @pl.when(first)
    def _():
        field[0] = opened[...]
        field[1] = opened[...]

    for side in range(2):
        faces_next[0, side] = (2.0 * robin_gain) * field[
            0, 8 * side : 8 * side + 8, own
        ] - hist[side, :, own]
    faces = face_copies(faces_next.at[0], faces_next.at[1], 2)
    start_faces(faces)

    lax.fori_loop(0, SMAX, functools.partial(stage, 1), 0)

    wide = exact(scatter_ref[...], field[SMAX % 2, :, own])
    for b in range(5):
        end_ref[0, :, b] = wide[:, plane(b)].reshape(px, 8, LANES)[:, :5]
    wait_faces(faces)
    for side, there in ((0, has_left), (1, has_right)):
        @pl.when(there)
        def _():
            for b in range(5):
                robin_ref[0, side, 0, b] = faces_next[1, side, 0:5, plane(b)]

        @pl.when(jnp.logical_not(there))
        def _():
            robin_ref[0, side, 0] = jnp.zeros(robin_ref.shape[3:], jnp.float32)


def solution(mesh):
    sizes = tuple(mesh.shape[name] for name in ("gx", "ta", "gy"))

    def local(initial_field, opening_guess, conductivity, capacity, section_count):
        px = initial_field.shape[0]
        tables = constants(px)
        count = len(row_order(px))
        slope_rows = tables[0].shape[0]
        total = PLANES * LANES
        f32 = jnp.float32
        vmem = pl.BlockSpec(memory_space=pltpu.VMEM)
        smem = pl.BlockSpec(memory_space=pltpu.SMEM)
        stages = ITERS * SMAX
        dma = pltpu.SemaphoreType.DMA
        return pl.pallas_call(
            functools.partial(kernel, sizes, step_size()),
            out_shape=(
                jax.ShapeDtypeStruct(opening_guess.shape, f32),
                jax.ShapeDtypeStruct((1, 2, 1) + initial_field.shape[1:], f32),
            ),
            in_specs=[vmem] * 4 + [smem] + [vmem] * 7 + [smem],
            out_specs=(vmem, vmem),
            scratch_shapes=[
                pltpu.VMEM((2, count, total), f32),
                pltpu.VMEM((count, total), f32),
                pltpu.VMEM((count, total), f32),
                pltpu.VMEM((count, total), f32),
                pltpu.VMEM((slope_rows, total), f32),
                pltpu.VMEM((count, total), f32),
                pltpu.VMEM((2, count, LANES), f32),
                pltpu.VMEM((px, 5, LANES), f32),
                pltpu.VMEM((3, px, 5, LANES), f32),
                pltpu.VMEM((stages, 2, count, LANES), f32),
                pltpu.VMEM((stages, 2, count, LANES), f32),
                pltpu.VMEM((2, 8, total), f32),
                pltpu.VMEM((2, 8, total), f32),
                pltpu.VMEM((2, 2, 8, 5 * LANES), f32),
                pltpu.VMEM((2, 8, total), f32),
                pltpu.VMEM((16, total), f32),
                dma((3,)), dma((3,)),
                dma((stages, 2)), dma((stages, 2)),
                dma((4,)), dma((4,)),
                dma, dma,
            ],
            compiler_params=pltpu.CompilerParams(
                collective_id=0, has_side_effects=True, vmem_limit_bytes=32 * 1024 * 1024
            ),
        )(
            initial_field, opening_guess, conductivity, capacity, section_count,
            *[jnp.asarray(t) for t in tables],
        )

    return jax.shard_map(
        local,
        mesh=mesh,
        in_specs=(
            P("gx", "gy", None, None),
            P("ta", "gx", "gy", None, None),
            P("gx", "gy", None, None),
            P("gx", "gy", None, None),
            P("gx"),
        ),
        out_specs=(P("ta", "gx", "gy", None, None), P("gx", None, "ta", "gy", None, None)),
        check_vma=False,
    )
```

time: 124 us -> 50.4 us (0.41)
  waiting for transfers between devices: 56.3 us -> 0 us
  Pallas kernels: 0 us -> 43.6 us
  starting transfers between devices: 23 us -> 0 us
  matrix products: 17.9 us -> 0 us
  local copies, waits for them, and re-layouts: 16.3 us -> 5.17 us
  other arithmetic: 5.8 us -> 0 us
  between operations: 3.97 us -> 1.38 us
    ppermute x22 -> x0, waiting for transfers between devices: 56.3 us -> none  [the longest x17 56.3 us: shifted_2(): return lax.ppermute(value, axis, pairs)]
    pallas_call x0 -> x1, Pallas kernels: none -> 43.6 us  [local(): pl.pallas_call(functools.partial(kernel, sizes, step_size()), out_shape=(...]
    ppermute x22 -> x0, starting transfers between devices: 23 us -> none  [the longest x5 13 us: shifted_3(): lax.ppermute(value, axis, [(source, source + steps) for source in range(l...]
    dot_general x48 -> x0, matrix products: 17.9 us -> none  [the longest x8 3.1 us: terms_third(): returned = jnp.einsum('ab,xyae->xybe', derivative, flux, precision=highest)]
    slice x79 -> x0, local copies, waits for them, and re-layouts: 4.06 us -> none  [the longest x11 1.77 us: along_first(): leading = field[:-1].reshape((element_count, 5) + field.shape[1:])]
    scatter-add x17 -> x0, local copies, waits for them, and re-layouts: 2.34 us -> none  [the longest x8 1.2 us: second_terms(): return interior.at[:, 0].add(arrived)]
    dot_general x23 -> x0, local copies, waits for them, and re-layouts: 2.17 us -> none  [the longest x8 1.4 us: terms_second(): jnp.einsum('ab,xea...->xeb...', derivative, flux, precision=highest)]
    unnamed x33 -> x26, local copies, waits for them, and re-layouts: 5.87 us -> 3.73 us
  transfers between devices with their start and end apart: 22 -> 0, of which waited for: 14 -> 0; matrix products, arithmetic and copies ran while one was open for 12% -> 0% of each run, Pallas kernels for 0% -> 0%
where the time goes in v1:
time: 50.4 us; the launch traced here: 50.2 us
  Pallas kernels  43.6 us (87%)
  local copies, waits for them, and re-layouts  5.17 us (10%)
  between operations  1.38 us (3%)
    pallas_call x1, Pallas kernels, local(): pl.pallas_call(functools.partial(kernel, sizes, step_size()), out_shape=(...  43.6 us
    unnamed x26, local copies, waits for them, and re-layouts  3.73 us
    pallas_call x2, local copies, waits for them, and re-layouts, local(): pl.pallas_call(functools.partial(kernel, sizes, step_size()), out_shape=(...  1.44 us

profile of v1, /device:TPU:0, one launch (start us, length us, event | category | flops | bytes accessed | tf_op | source)
XLA Modules:
  0.0 50.2 jit_solution(10298049416110346734)
XLA Ops:
  1.3 0.0 copy-start.10
  1.3 1.0 %copy.15.init_ref = f32[11,5,5,128]{3,2,1,0:T(8,128)S(1)} copy(f32[11,5,5,128]{3,0,2,1:T(8,128)} %param.13) | data formatting | bytes 281600 | tf_op args[0]
  2.3 0.0 copy-done.10
  2.3 0.0 copy-start.8
  2.4 0.9 %copy-done.8 = f32[11,5,5,128]{3,0,2,1:T(8,128)S(1)} copy-done((f32[11,5,5,128]{3,0,2,1:T(8,128)S(1)}, f32[11,5,5,128]{3,0,2,1:T(8,128)}, u32[]{:S(2)}) %copy-start.8) | copy-done | bytes 140824
  3.3 0.0 copy-start.9
  3.3 0.1 copy.17.cond_ref
  3.3 0.9 %copy-done.9 = f32[11,5,5,128]{3,0,2,1:T(8,128)S(1)} copy-done((f32[11,5,5,128]{3,0,2,1:T(8,128)S(1)}, f32[11,5,5,128]{3,0,2,1:T(8,128)}, u32[]{:S(2)}) %copy-start.9) | copy-done | bytes 140824
  4.2 0.0 copy-start
  4.2 0.0 copy-start.1
  4.2 0.0 copy-start.2
  4.2 0.0 copy-start.3
  4.2 0.0 copy-start.4
  4.2 0.0 copy-start.5
  4.2 0.0 copy-start.6
  4.2 0.0 copy-start.7
  4.3 0.1 copy.18.cap_ref
  4.3 0.7 %copy-done = bf16[128,240]{1,0:T(8,128)(2,1)S(1)} copy-done((bf16[128,240]{1,0:T(8,128)(2,1)S(1)}, bf16[128,240]{1,0:T(8,128)(2,1)}, u32[]{:S(2)}) %copy-start) | copy-done | bytes 61464
  5.0 0.0 copy-done.1
  5.1 0.0 copy-done.2
  5.1 0.0 copy-done.3
  5.1 0.0 copy-done.4
  5.1 0.0 copy-done.5
  5.1 0.0 copy-done.6
  5.1 0.0 copy-done.7
  5.1 43.6 %shard_map.140 = (f32[1,11,5,5,128]{4,3,2,1,0:T(8,128)S(1)}, f32[1,2,1,5,5,128]{5,4,3,2,1,0:T(8,128)S(1)}) custom-call(f32[11,5,5,128]{3,2,1,0:T(8,128)S(1)} %copy.15.init_ref, f32[1,11,5,5,128]{4,3,2,1,0:T(8,128)S(1)} %copy.16.guess_ref, f32[11,5,5,128]{3,2,1,0:T(8,128)S(1)} %copy.17.cond_ref, f32[11,5,5,128]{3,2,1,0:T(8,128)S(1)} %copy.18.cap_ref, ...), custom_call_target="tpu_custom_call" | custom-call | tf_op jit(solution)/shard_map/pallas_call | solution.py:460
  48.7 0.8 %copy.19 = f32[1,11,5,5,128]{4,0,3,2,1:T(1,128)} copy(f32[1,11,5,5,128]{4,3,2,1,0:T(8,128)S(1)} %get-tuple-element.2) | data formatting | bytes 281600 | tf_op jit(solution)/shard_map/pallas_call | solution.py:460
  49.5 0.6 %copy.20 = f32[1,2,1,5,5,128]{5,2,4,3,1,0:T(1,128)} copy(f32[1,2,1,5,5,128]{5,4,3,2,1,0:T(8,128)S(1)} %get-tuple-element.3) | data formatting | bytes 51200 | tf_op jit(solution)/shard_map/pallas_call | solution.py:460
  (1 shorter events, 0.0 us)
Async XLA Ops:
  1.3 1.0 %copy-start.10 = (f32[1,11,5,5,128]{4,0,3,2,1:T(1,128)S(1)}, f32[1,11,5,5,128]{4,0,3,2,1:T(1,128)}, u32[]{:S(2)}) copy-start(f32[1,11,5,5,128]{4,0,3,2,1:T(1,128)} %param.14) | copy-start | bytes 422404
  2.3 0.9 %copy-start.8 = (f32[11,5,5,128]{3,0,2,1:T(8,128)S(1)}, f32[11,5,5,128]{3,0,2,1:T(8,128)}, u32[]{:S(2)}) copy-start(f32[11,5,5,128]{3,0,2,1:T(8,128)} %param.15) | copy-start | bytes 422404
  3.3 0.9 %copy-start.9 = (f32[11,5,5,128]{3,0,2,1:T(8,128)S(1)}, f32[11,5,5,128]{3,0,2,1:T(8,128)}, u32[]{:S(2)}) copy-start(f32[11,5,5,128]{3,0,2,1:T(8,128)} %param.16) | copy-start | bytes 422404
  4.2 0.8 %copy-start = (bf16[128,240]{1,0:T(8,128)(2,1)S(1)}, bf16[128,240]{1,0:T(8,128)(2,1)}, u32[]{:S(2)}) copy-start(bf16[128,240]{1,0:T(8,128)(2,1)} %constant.18.clone.spread_ref) | copy-start | bytes 184324
  4.2 0.9 %copy-start.1 = (bf16[128,240]{1,0:T(8,128)(2,1)S(1)}, bf16[128,240]{1,0:T(8,128)(2,1)}, u32[]{:S(2)}) copy-start(bf16[128,240]{1,0:T(8,128)(2,1)} %constant.16.clone.slope_ref) | copy-start | bytes 184324
  4.2 0.9 %copy-start.2 = (bf16[80,384]{1,0:T(8,128)(2,1)S(1)}, bf16[80,384]{1,0:T(8,128)(2,1)}, u32[]{:S(2)}) copy-start(bf16[80,384]{1,0:T(8,128)(2,1)} %constant.17.clone.back_ref) | copy-start | bytes 184324
  4.2 0.9 %copy-start.3 = (f32[88,56]{1,0:T(8,128)S(1)}, f32[88,56]{1,0:T(8,128)}, u32[]{:S(2)}) copy-start(f32[88,56]{1,0:T(8,128)} %constant.20.clone.scatter_ref) | copy-start | bytes 59140
  4.2 0.9 %copy-start.4 = (f32[56,128]{1,0:T(8,128)S(1)}, f32[56,128]{1,0:T(8,128)}, u32[]{:S(2)}) copy-start(f32[56,128]{1,0:T(8,128)} %constant.21.clone.weight_ref) | copy-start | bytes 86020
  4.2 0.9 %copy-start.5 = (f32[56,88]{1,0:T(8,128)S(1)}, f32[56,88]{1,0:T(8,128)}, u32[]{:S(2)}) copy-start(f32[56,88]{1,0:T(8,128)} %constant.19.clone.gather_ref) | copy-start | bytes 59140
  4.2 0.9 %copy-start.6 = (f32[16,128]{1,0:T(8,128)S(1)}, f32[16,128]{1,0:T(8,128)}, u32[]{:S(2)}) copy-start(f32[16,128]{1,0:T(8,128)} %constant.22.clone.face_ref) | copy-start | bytes 24580
  4.2 0.9 %copy-start.7 = (f32[2,12]{1,0:T(2,128)S(1)}, f32[2,12]{1,0:T(2,128)}, u32[]{:S(2)}) copy-start(f32[2,12]{1,0:T(2,128)} %constant.23.clone.table_ref) | copy-start | bytes 292

commit v2 on v1

v2 whole, which is shorter than its diff:
```python
import functools
import math

import jax
import jax.numpy as jnp
import ml_dtypes
import numpy as np
from jax import lax
from jax.experimental import pallas as pl
from jax.experimental.pallas import tpu as pltpu
from jax.sharding import PartitionSpec as P

ITERS = 2
SMIN = 3
SMAX = 4
LANES = 128
MESH = pl.DeviceIdType.MESH

robin_gain = 2.0
kappa_top = 2.0
capacity_low = 0.5
damping = 0.05


def gll_tables():
    root_seven = math.sqrt(7.0)
    outer = math.sqrt(1.0 / 3.0 + 2.0 * root_seven / 21.0)
    closer = math.sqrt(1.0 / 3.0 - 2.0 * root_seven / 21.0)
    points = np.array([-1.0, -outer, -closer, closer, outer, 1.0])
    low, high = (14.0 - root_seven) / 30.0, (14.0 + root_seven) / 30.0
    weights = np.array([1.0 / 15.0, low, high, high, low, 1.0 / 15.0])
    products = np.array(
        [np.prod([points[i] - points[k] for k in range(6) if k != i]) for i in range(6)]
    )
    derivative = np.zeros((6, 6))
    for i in range(6):
        for k in range(6):
            if i != k:
                derivative[i, k] = products[i] / (products[k] * (points[i] - points[k]))
    for i in range(6):
        derivative[i, i] = -derivative[i].sum()
    return (points, weights, derivative)


def line_weights(count, closed):
    weights = gll_tables()[1]
    pattern = np.array([weights[i % 5] if i % 5 else 2.0 * weights[0] for i in range(count)])
    if closed:
        pattern[0] = weights[0]
        pattern[-1] = weights[0]
    return pattern


def step_size():
    points, weights, derivative = gll_tables()
    row_sums = np.abs(derivative).sum(axis=1)
    gersh_bound = max(
        float(np.sum(np.abs(derivative[:, i]) * weights * row_sums) / weights[i]) for i in range(6)
    )
    spectral = kappa_top / capacity_low * 3.0 * gersh_bound + robin_gain / (
        capacity_low * weights[0]
    )
    return float(0.8 * 1.93 * SMIN**2 / spectral)


def rkc_table(sections):
    shifted = 1.0 + damping / sections**2
    cheb, derivs = [1.0, shifted], [0.0, 1.0]
    for j in range(2, SMAX + 1):
        cheb.append(2.0 * shifted * cheb[-1] - cheb[-2])
        derivs.append(2.0 * cheb[j - 1] + 2.0 * shifted * derivs[j - 1] - derivs[j - 2])
    spread = cheb[sections] / derivs[sections]
    rows = [(1.0, 0.0, spread / shifted)]
    for j in range(2, SMAX + 1):
        if j <= sections:
            rows.append(
                (
                    2.0 * shifted * cheb[j - 1] / cheb[j],
                    -cheb[j - 2] / cheb[j],
                    2.0 * spread * cheb[j - 1] / cheb[j],
                )
            )
        else:
            rows.append((1.0, 0.0, 0.0))
    return np.array(rows)


def stacked(matrix):
    matrix = matrix.astype(np.float32)
    high = matrix.astype(ml_dtypes.bfloat16)
    low = (matrix - high.astype(np.float32)).astype(ml_dtypes.bfloat16)
    return np.concatenate([high, high, low], axis=1)


def row_order(px):
    inner = list(range(1, px - 1))
    first, second, third = inner[:3], inner[3:6], inner[6:]
    rows = [(0, q) for q in range(5)] + [(x, 0) for x in first]
    rows += [(px - 1, q) for q in range(5)] + [(x, 0) for x in second]
    rows += [(x, 0) for x in third]
    rows += [(x, q) for x in inner for q in range(1, 5)]
    while len(rows) % 8:
        rows.append((1, 1))
    return rows


LEAD = 24


def constants(px):
    points, quad, deriv = gll_tables()
    wx, wz = line_weights(px, True), line_weights(5, False)
    rows = row_order(px)
    count = len(rows)
    place = {}
    for r, node in enumerate(rows):
        place.setdefault(node, r)
    elements = (px - 1) // 5
    slope_rows = elements * 30 + px * 6
    padded = -(-slope_rows // 16) * 16
    slope = np.zeros((padded, count + LEAD))
    spread = np.zeros((padded, count + LEAD))
    r = 0
    for e in range(elements):
        for a in range(6):
            for q in range(5):
                for b in range(6):
                    slope[r, place[5 * e + b, q]] = deriv[a, b]
                spread[r, place[5 * e + a, q]] = quad[a] * wz[q]
                r += 1
    for x in range(px):
        for a in range(6):
            for b in range(5):
                slope[r, place[x, b]] = deriv[a, b]
            slope[r, count + place[x, 0]] = deriv[a, 5]
            source = place[x, a] if a < 5 else count + place[x, 0]
            spread[r, source] = quad[a] * wx[x]
            r += 1
    high = -(-px // 8) * 8
    gather = np.zeros((count, 5 * high), np.float32)
    scatter = np.zeros((px * 8, count), np.float32)
    for r, (x, q) in enumerate(rows):
        gather[r, high * q + x] = 1.0
    for (x, q), r in place.items():
        scatter[8 * x + q, r] = 1.0
    ones = np.ones((1, LANES))
    weight = np.array([wx[x] * wz[q] for x, q in rows])[:, None] * ones
    face = np.zeros((16, 1))
    face[0:5, 0] = wz
    face[8:13, 0] = wz
    table = np.stack([rkc_table(s).reshape(-1) for s in range(SMIN, SMAX + 1)])
    f32 = np.float32
    return (
        stacked(slope),
        stacked(slope.T),
        stacked(spread),
        gather,
        scatter,
        weight.astype(f32),
        (face * ones).astype(f32),
        table.astype(f32),
    )


def halves(value):
    high = value.astype(jnp.bfloat16)
    low = (value - high.astype(jnp.float32)).astype(jnp.bfloat16)
    return jnp.concatenate([high, low, high], axis=0)


def product(matrix, value):
    return jnp.dot(matrix, halves(value), preferred_element_type=jnp.float32)


def exact(matrix, value):
    return jnp.dot(
        matrix, value, preferred_element_type=jnp.float32, precision=lax.Precision.HIGHEST
    )


def plane(b):
    return slice(LANES * b, LANES * (b + 1))


def rolled(value, shift):
    parts = value.shape[1] // LANES
    return jnp.concatenate(
        [pltpu.roll(value[:, plane(b)], shift % LANES, 1) for b in range(parts)], axis=1
    )


def extended(value):
    return jnp.concatenate([value, rolled(value[:LEAD], -1)], axis=0)


def wide_rows(ref):
    px = ref.shape[2]
    extra = -px % 8
    zeros = jnp.zeros((5, extra, LANES), jnp.float32)
    return [
        jnp.concatenate([ref[b], zeros], axis=1).reshape(5 * (px + extra), LANES)
        for b in range(5)
    ]


def kernel(
    sizes,
    step_len,
    init_ref, guess_ref, cond_ref, cap_ref, sec_ref,
    slope_ref, back_ref, spread_ref, gather_ref, scatter_ref, weight_ref, face_ref, table_ref,
    end_ref, robin_ref,
    field, inputs, inv, flux_x, flux_y, y_terms, spill, packs, ends_in,
    faces_out, faces_in, robin_out, robin_in, hist, drive,
    in_send, in_recv, f_send, f_recv, r_send, r_recv, e_send, e_recv,
):
    n_gx, n_ta, n_gy = sizes
    quad, deriv = gll_tables()[1:]
    deriv = [[float(v) for v in row] for row in deriv]
    wy = [float(2.0 * quad[0])] + [float(quad[b]) for b in range(1, 5)]
    gx, ta, gy = lax.axis_index("gx"), lax.axis_index("ta"), lax.axis_index("gy")
    after, before = lax.rem(ta + 1, n_ta), lax.rem(ta + n_ta - 1, n_ta)
    low_hub, hubs = (n_gy - 1) // 2, 1 if n_gy == 1 else 2

    def hub_of(block):
        return low_hub + lax.rem(block, hubs)

    hub, hub_before = hub_of(ta), hub_of(before)
    is_hub = gy == hub
    sides = ((gx > 0, gx - 1), (gx < n_gx - 1, gx + 1))
    px = init_ref.shape[2]

    barrier = pltpu.get_barrier_semaphore()

    def greet(x, t, y):
        pl.semaphore_signal(
            barrier, inc=1, device_id={"gx": x, "ta": t, "gy": y}, device_id_type=MESH
        )

    neighbours = sides[0][0].astype(jnp.int32) + sides[1][0].astype(jnp.int32)
    greet(gx, before, hub_before)
    for there, x in sides:
        pl.when(there)(functools.partial(greet, x, before, hub_before))
    pl.when(jnp.logical_not(is_hub))(functools.partial(greet, gx, ta, hub))

    @pl.when(is_hub)
    def _():
        for p in range(n_gy):
            pl.when(gy != p)(functools.partial(greet, gx, ta, p))
            greet(gx, after, p)
            for there, x in sides:
                pl.when(there)(functools.partial(greet, x, after, p))

    gather = gather_ref[...]
    first = ta == 0
    starts_first = jnp.logical_or(first, ta == n_ta - 1)
    fresh, guess = wide_rows(init_ref), wide_rows(guess_ref)

    def chosen(there):
        return jnp.concatenate(
            [jnp.where(there, fresh[b], guess[b]) for b in range(5)], axis=1
        )

    packs[0] = exact(gather, jnp.concatenate(wide_rows(cond_ref), axis=1))
    packs[1] = exact(gather, jnp.concatenate(wide_rows(cap_ref), axis=1))
    packs[2] = exact(gather, chosen(starts_first))
    own_faces = exact(gather[:16], chosen(first))
    faces_out[0] = own_faces[:8]
    faces_out[1] = own_faces[8:]

    pl.semaphore_wait(
        barrier,
        2 + neighbours + is_hub.astype(jnp.int32) * (2 * n_gy - 2 + n_gy * neighbours),
    )

    def input_copy(k):
        return pltpu.make_async_remote_copy(
            src_ref=packs.at[k], dst_ref=inputs.at[k, gy], send_sem=in_send.at[k],
            recv_sem=in_recv.at[k, gy], device_id={"gy": hub}, device_id_type=MESH,
        )

    def face_copy(side):
        return pltpu.make_async_remote_copy(
            src_ref=faces_out.at[side], dst_ref=faces_in.at[1 - side, gy],
            send_sem=f_send.at[side], recv_sem=f_recv.at[1 - side, gy],
            device_id={"gx": sides[side][1], "ta": before, "gy": hub_before},
            device_id_type=MESH,
        )

    def end_copy(p):
        return pltpu.make_async_remote_copy(
            src_ref=field.at[SMAX % 2, p], dst_ref=ends_in, send_sem=e_send.at[p],
            recv_sem=e_recv, device_id={"ta": after, "gy": p}, device_id_type=MESH,
        )

    def robin_copy(side, p):
        return pltpu.make_async_remote_copy(
            src_ref=robin_out.at[side, p], dst_ref=robin_in.at[1 - side],
            send_sem=r_send.at[side, p], recv_sem=r_recv.at[1 - side],
            device_id={"gx": sides[side][1], "ta": after, "gy": p}, device_id_type=MESH,
        )

    @pl.when(jnp.logical_not(is_hub))
    def _():
        for k in range(3):
            input_copy(k).start()

    for side in range(2):
        pl.when(sides[side][0])(face_copy(side).start)

    @pl.when(is_hub)
    def _():
        for k in range(3):
            inputs[k, gy] = packs[k]
        weight, face = weight_ref[...], face_ref[...]

        def wait_inputs(k, p):
            def arrival():
                pltpu.make_async_copy(packs.at[k], inputs.at[k, p], in_recv.at[k, p]).wait()

            pl.when(gy != p)(arrival)

        for p in range(n_gy):
            wait_inputs(0, p)
            kappa = inputs[0, p]
            spread_out = product(spread_ref[...], extended(kappa))
            for b in range(5):
                flux_x[p, :, plane(b)] = spread_out[:, plane(b)] * wy[b]
                flux_y[p, :, plane(b)] = kappa[:, plane(b)] * weight * float(quad[b])
        for p in range(n_gy):
            wait_inputs(1, p)
            for b in range(5):
                inv[p, :, plane(b)] = (step_len / wy[b]) / (inputs[1, p, :, plane(b)] * weight)
        for p in range(n_gy):
            wait_inputs(2, p)
            field[0, p] = inputs[2, p]
            field[1, p] = inputs[2, p]
            drive[p] = jnp.zeros(drive.shape[1:], jnp.float32)

        sections = sec_ref[0]

        def coefficient(j, k):
            value = table_ref[0, 3 * j + k]
            for s in range(1, SMAX - SMIN + 1):
                value = jnp.where(sections == SMIN + s, table_ref[s, 3 * j + k], value)
            return value

        def combine(terms):
            total = terms[0]
            for term in terms[1:]:
                total = total + term
            return total

        def stage(j, carry):
            now = lax.rem(j, 2)
            later = 1 - now
            mu, nu, tilde = (coefficient(j, k) for k in range(3))
            for p in range(n_gy):
                behind = (p + 1) % n_gy
                u = [field[now, p, :, plane(b)] for b in range(5)]
                u.append(field[now, behind, :, plane(0)])
                weights = [flux_y[p, :, plane(b)] for b in range(5)]
                weights.append(flux_y[behind, :, plane(0)])
                flux = [
                    weights[a] * combine([deriv[a][b] * u[b] for b in range(6)])
                    for a in range(6)
                ]
                for b in range(6):
                    value = combine([deriv[a][b] * flux[a] for a in range(6)])
                    if b < 5:
                        y_terms[p, :, plane(b)] = value
                    else:
                        spill[p] = value
            for p in range(n_gy):
                whole = field[now, p]
                count = whole.shape[0]
                slopes = product(slope_ref[...], extended(whole))
                back = product(back_ref[...], slopes * flux_x[p])
                wrapped = rolled(back[count:], 1)
                for b in range(5):
                    u = field[now, p, :, plane(b)]
                    value = back[:count, plane(b)] + y_terms[p, :, plane(b)]
                    if b == 0:
                        value = value + spill[(p - 1) % n_gy]
                    lead = value[:LEAD] + wrapped[:, plane(b)]
                    top = lead[:16] + face * (robin_gain * wy[b]) * u[:16]
                    top = top - drive[p, :, plane(b)]
                    total = jnp.concatenate([top, lead[16:], value[LEAD:]], axis=0)
                    field[later, p, :, plane(b)] = (
                        mu * u
                        + nu * field[later, p, :, plane(b)]
                        - tilde * (inv[p, :, plane(b)] * total)
                    )
            return carry

        lax.fori_loop(0, SMAX, stage, 0)

        for side in range(2):
            there = sides[side][0]

            @pl.when(there)
            def _():
                for p in range(n_gy):
                    pltpu.make_async_copy(
                        faces_out.at[side], faces_in.at[side, p], f_recv.at[side, p]
                    ).wait()
                    hist[side, p] = (2.0 * robin_gain) * faces_in[side, p]

            @pl.when(jnp.logical_not(there))
            def _():
                hist[side] = jnp.zeros(hist.shape[1:], jnp.float32)

        @pl.when(ta == n_ta - 1)
        def _():
            field[0] = inputs[2]

        for p in range(n_gy):
            field[1, p] = field[0, p]
            for side in range(2):
                rows = slice(8 * side, 8 * side + 8)
                known = hist[side, p]
                robin_out[side, p] = (2.0 * robin_gain) * field[0, p, rows] - known
                for b in range(5):
                    drive[p, rows, plane(b)] = face[rows] * wy[b] * known[:, plane(b)]
        for side in range(2):
            @pl.when(sides[side][0])
            def _():
                for p in range(n_gy):
                    robin_copy(side, p).start()

        lax.fori_loop(0, SMAX, stage, 0)

        for p in range(n_gy):
            end_copy(p).start()

    @pl.when(jnp.logical_not(is_hub))
    def _():
        for k in range(3):
            input_copy(k).wait_send()

    for side in range(2):
        there = sides[side][0]
        pl.when(there)(face_copy(side).wait_send)

        @pl.when(there)
        def _():
            pltpu.make_async_copy(
                faces_out.at[side], robin_in.at[side], r_recv.at[side]
            ).wait()
            for b in range(5):
                robin_ref[0, side, 0, b] = robin_in[side, 0:5, plane(b)]

        @pl.when(jnp.logical_not(there))
        def _():
            robin_ref[0, side, 0] = jnp.zeros(robin_ref.shape[3:], jnp.float32)

    pltpu.make_async_copy(packs.at[0], ends_in, e_recv).wait()
    wide = exact(scatter_ref[...], ends_in[...])
    for b in range(5):
        end_ref[0, :, b] = wide[:, plane(b)].reshape(px, 8, LANES)[:, :5]

    @pl.when(is_hub)
    def _():
        for side in range(2):
            @pl.when(sides[side][0])
            def _():
                for p in range(n_gy):
                    robin_copy(side, p).wait_send()
        for p in range(n_gy):
            end_copy(p).wait_send()


def solution(mesh):
    sizes = tuple(mesh.shape[name] for name in ("gx", "ta", "gy"))
    n_gy = sizes[2]

    def local(initial_field, opening_guess, conductivity, capacity, section_count):
        px = initial_field.shape[0]
        tables = constants(px)
        count = len(row_order(px))
        slope_rows = tables[0].shape[0]
        wide = 5 * LANES
        f32 = jnp.float32
        vmem = pl.BlockSpec(memory_space=pltpu.VMEM)
        smem = pl.BlockSpec(memory_space=pltpu.SMEM)
        dma = pltpu.SemaphoreType.DMA
        moved = [
            jnp.transpose(a, (1, 2, 0, 3))
            for a in (initial_field, opening_guess[0], conductivity, capacity)
        ]
        ring = (n_gy, count, wide)
        shapes = [
            (2,) + ring, (3,) + ring, ring, (n_gy, slope_rows, wide), ring, ring,
            (n_gy, count, LANES), (3, count, wide), (count, wide),
            (2, 8, wide), (2, n_gy, 8, wide), (2, n_gy, 8, wide), (2, 8, wide),
            (2, n_gy, 8, wide), (n_gy, 16, wide),
        ]
        return pl.pallas_call(
            functools.partial(kernel, sizes, step_size()),
            out_shape=(
                jax.ShapeDtypeStruct(opening_guess.shape, f32),
                jax.ShapeDtypeStruct((1, 2, 1) + initial_field.shape[1:], f32),
            ),
            in_specs=[vmem] * 4 + [smem] + [vmem] * 7 + [smem],
            out_specs=(vmem, vmem),
            scratch_shapes=[pltpu.VMEM(shape, f32) for shape in shapes]
            + [
                dma((3,)), dma((3, n_gy)), dma((2,)), dma((2, n_gy)),
                dma((2, n_gy)), dma((2,)), dma((n_gy,)), dma,
            ],
            compiler_params=pltpu.CompilerParams(
                collective_id=0, has_side_effects=True, vmem_limit_bytes=32 * 1024 * 1024
            ),
        )(*moved, section_count, *[jnp.asarray(t) for t in tables])

    return jax.shard_map(
        local,
        mesh=mesh,
        in_specs=(
            P("gx", "gy", None, None),
            P("ta", "gx", "gy", None, None),
            P("gx", "gy", None, None),
            P("gx", "gy", None, None),
            P("gx"),
        ),
        out_specs=(P("ta", "gx", "gy", None, None), P("gx", None, "ta", "gy", None, None)),
        check_vma=False,
    )
```

time: 50.4 us -> 43.9 us (0.87)
  Pallas kernels: 43.6 us -> 34 us
  local copies, waits for them, and re-layouts: 5.17 us -> 8.04 us
    pallas_call x1, Pallas kernels: 43.6 us -> 34 us  [local(): pl.pallas_call(functools.partial(kernel, sizes, step_size()), out_shape=(...]
    unnamed x26 -> x23, local copies, waits for them, and re-layouts: 3.73 us -> 6.6 us
where the time goes in v2:
time: 43.9 us; the launch traced here: 43.5 us
  Pallas kernels  34 us (77%)
  local copies, waits for them, and re-layouts  8.04 us (18%)
  between operations  1.41 us (3%)
    pallas_call x1, Pallas kernels, local(): pl.pallas_call(functools.partial(kernel, sizes, step_size()), out_shape=(...  34 us
    unnamed x23, local copies, waits for them, and re-layouts  6.6 us
    pallas_call x2, local copies, waits for them, and re-layouts, local(): pl.pallas_call(functools.partial(kernel, sizes, step_size()), out_shape=(...  1.44 us

profile of v2, /device:TPU:0, one launch (start us, length us, event | category | flops | bytes accessed | tf_op | source)
XLA Modules:
  0.0 43.5 jit_solution(13066727174679587472)
XLA Ops:
  0.6 0.0 copy-start
  1.3 0.0 copy-start.3
  1.3 0.0 copy-start.4
  1.4 0.0 copy-start.9
  1.4 1.0 %copy.19 = f32[1,11,5,5,128]{4,1,3,2,0:T(8,128)S(1)} copy(f32[1,11,5,5,128]{4,0,3,2,1:T(1,128)} %param.14) | data formatting | bytes 281600 | tf_op args[1]
  2.3 0.0 copy-start.10
  2.4 0.0 copy-done
  2.4 0.0 copy-done.3
  2.4 0.0 copy-done.4
  2.4 0.0 copy-done.9
  2.4 0.6 %copy-done.10 = f32[2,12]{1,0:T(2,128)S(1)} copy-done((f32[2,12]{1,0:T(2,128)S(1)}, f32[2,12]{1,0:T(2,128)}, u32[]{:S(2)}) %copy-start.10) | copy-done | bytes 120
  3.0 0.0 copy-start.1
  3.0 0.9 %copy-done.1 = f32[11,5,5,128]{3,0,2,1:T(8,128)S(1)} copy-done((f32[11,5,5,128]{3,0,2,1:T(8,128)S(1)}, f32[11,5,5,128]{3,0,2,1:T(8,128)}, u32[]{:S(2)}) %copy-start.1) | copy-done | bytes 140824
  4.0 0.0 copy-start.2
  4.0 0.9 %copy-done.2 = f32[11,5,5,128]{3,0,2,1:T(8,128)S(1)} copy-done((f32[11,5,5,128]{3,0,2,1:T(8,128)S(1)}, f32[11,5,5,128]{3,0,2,1:T(8,128)}, u32[]{:S(2)}) %copy-start.2) | copy-done | bytes 140824
  4.9 0.0 copy-start.5
  4.9 0.8 %copy-done.5 = bf16[80,384]{1,0:T(8,128)(2,1)S(1)} copy-done((bf16[80,384]{1,0:T(8,128)(2,1)S(1)}, bf16[80,384]{1,0:T(8,128)(2,1)}, u32[]{:S(2)}) %copy-start.5) | copy-done | bytes 61464
  5.7 0.0 copy-start.6
  5.7 0.8 %copy-done.6 = f32[88,56]{1,0:T(8,128)S(1)} copy-done((f32[88,56]{1,0:T(8,128)S(1)}, f32[88,56]{1,0:T(8,128)}, u32[]{:S(2)}) %copy-start.6) | copy-done | bytes 19736
  6.5 0.0 copy-start.7
  6.5 0.7 %copy-done.7 = f32[56,128]{1,0:T(8,128)S(1)} copy-done((f32[56,128]{1,0:T(8,128)S(1)}, f32[56,128]{1,0:T(8,128)}, u32[]{:S(2)}) %copy-start.7) | copy-done | bytes 28696
  7.2 0.0 copy-start.8
  7.3 0.7 %copy-done.8 = f32[56,80]{1,0:T(8,128)S(1)} copy-done((f32[56,80]{1,0:T(8,128)S(1)}, f32[56,80]{1,0:T(8,128)}, u32[]{:S(2)}) %copy-start.8) | copy-done | bytes 17944
  8.0 34.0 %shard_map.140 = (f32[1,11,5,5,128]{4,3,2,1,0:T(8,128)S(1)}, f32[1,2,1,5,5,128]{5,4,3,2,1,0:T(8,128)S(1)}) custom-call(f32[5,5,11,128]{3,2,1,0:T(8,128)S(1)} %bitcast.9, f32[5,5,11,128]{3,2,1,0:T(8,128)S(1)} %bitcast.8, f32[5,5,11,128]{3,2,1,0:T(8,128)S(1)} %bitcast.10, f32[5,5,11,128]{3,2,1,0:T(8,128)S(1)} %bitcast.11, s32[1]{0:T(128)S(6)} %copy.20.sec_ref, ...), custom_call_target="tpu_custom_call" | custom-call | tf_op jit(solution)/shard_map/pallas_call | solution.py:497
  42.0 0.8 %copy.16 = f32[1,11,5,5,128]{4,0,3,2,1:T(1,128)} copy(f32[1,11,5,5,128]{4,3,2,1,0:T(8,128)S(1)} %get-tuple-element.2) | data formatting | bytes 281600 | tf_op jit(solution)/shard_map/pallas_call | solution.py:497
  42.8 0.6 %copy.17 = f32[1,2,1,5,5,128]{5,2,4,3,1,0:T(1,128)} copy(f32[1,2,1,5,5,128]{5,4,3,2,1,0:T(8,128)S(1)} %get-tuple-element.3) | data formatting | bytes 51200 | tf_op jit(solution)/shard_map/pallas_call | solution.py:497
Async XLA Ops:
  0.6 1.7 %copy-start = (f32[11,5,5,128]{3,0,2,1:T(8,128)S(1)}, f32[11,5,5,128]{3,0,2,1:T(8,128)}, u32[]{:S(2)}) copy-start(f32[11,5,5,128]{3,0,2,1:T(8,128)} %param.13) | copy-start | bytes 422404
  1.3 1.0 %copy-start.3 = (bf16[128,240]{1,0:T(8,128)(2,1)S(1)}, bf16[128,240]{1,0:T(8,128)(2,1)}, u32[]{:S(2)}) copy-start(bf16[128,240]{1,0:T(8,128)(2,1)} %constant.18.clone.spread_ref) | copy-start | bytes 184324
  1.3 1.0 %copy-start.4 = (bf16[128,240]{1,0:T(8,128)(2,1)S(1)}, bf16[128,240]{1,0:T(8,128)(2,1)}, u32[]{:S(2)}) copy-start(bf16[128,240]{1,0:T(8,128)(2,1)} %constant.16.clone.slope_ref) | copy-start | bytes 184324
  1.4 1.0 %copy-start.9 = (f32[16,128]{1,0:T(8,128)S(1)}, f32[16,128]{1,0:T(8,128)}, u32[]{:S(2)}) copy-start(f32[16,128]{1,0:T(8,128)} %constant.22.clone.face_ref) | copy-start | bytes 24580
  2.3 0.7 %copy-start.10 = (f32[2,12]{1,0:T(2,128)S(1)}, f32[2,12]{1,0:T(2,128)}, u32[]{:S(2)}) copy-start(f32[2,12]{1,0:T(2,128)} %constant.23.clone.table_ref) | copy-start | bytes 292
  3.0 0.9 %copy-start.1 = (f32[11,5,5,128]{3,0,2,1:T(8,128)S(1)}, f32[11,5,5,128]{3,0,2,1:T(8,128)}, u32[]{:S(2)}) copy-start(f32[11,5,5,128]{3,0,2,1:T(8,128)} %param.15) | copy-start | bytes 422404
  4.0 0.9 %copy-start.2 = (f32[11,5,5,128]{3,0,2,1:T(8,128)S(1)}, f32[11,5,5,128]{3,0,2,1:T(8,128)}, u32[]{:S(2)}) copy-start(f32[11,5,5,128]{3,0,2,1:T(8,128)} %param.16) | copy-start | bytes 422404
  4.9 0.8 %copy-start.5 = (bf16[80,384]{1,0:T(8,128)(2,1)S(1)}, bf16[80,384]{1,0:T(8,128)(2,1)}, u32[]{:S(2)}) copy-start(bf16[80,384]{1,0:T(8,128)(2,1)} %constant.17.clone.back_ref) | copy-start | bytes 184324
  5.7 0.8 %copy-start.6 = (f32[88,56]{1,0:T(8,128)S(1)}, f32[88,56]{1,0:T(8,128)}, u32[]{:S(2)}) copy-start(f32[88,56]{1,0:T(8,128)} %constant.20.clone.scatter_ref) | copy-start | bytes 59140
  6.5 0.7 %copy-start.7 = (f32[56,128]{1,0:T(8,128)S(1)}, f32[56,128]{1,0:T(8,128)}, u32[]{:S(2)}) copy-start(f32[56,128]{1,0:T(8,128)} %constant.21.clone.weight_ref) | copy-start | bytes 86020
  7.2 0.7 %copy-start.8 = (f32[56,80]{1,0:T(8,128)S(1)}, f32[56,80]{1,0:T(8,128)}, u32[]{:S(2)}) copy-start(f32[56,80]{1,0:T(8,128)} %constant.19.clone.gather_ref) | copy-start | bytes 53764

commit v3 on v2

--- a/solution.py
+++ b/solution.py
@@ -148,17 +148,14 @@
     face = np.zeros((16, 1))
     face[0:5, 0] = wz
     face[8:13, 0] = wz
-    table = np.stack([rkc_table(s).reshape(-1) for s in range(SMIN, SMAX + 1)])
     f32 = np.float32
     return (
-        stacked(slope),
-        stacked(slope.T),
-        stacked(spread),
+        np.stack([stacked(slope), stacked(spread)]).astype(f32),
+        stacked(slope.T).astype(f32),
         gather,
         scatter,
         weight.astype(f32),
         (face * ones).astype(f32),
-        table.astype(f32),
     )
 
 
@@ -206,16 +203,19 @@
 def kernel(
     sizes,
     step_len,
-    init_ref, guess_ref, cond_ref, cap_ref, sec_ref,
-    slope_ref, back_ref, spread_ref, gather_ref, scatter_ref, weight_ref, face_ref, table_ref,
+    init_hbm, guess_hbm, cond_hbm, cap_hbm, sec_ref,
+    forward_hbm, back_hbm, gather_hbm, scatter_hbm, weight_hbm, face_hbm,
     end_ref, robin_ref,
+    init_ref, guess_ref, cond_ref, cap_ref,
+    forward_ref, back_ref, gather_ref, scatter_ref, weight_ref, face_ref, load_sem,
     field, inputs, inv, flux_x, flux_y, y_terms, spill, packs, ends_in,
     faces_out, faces_in, robin_out, robin_in, hist, drive,
     in_send, in_recv, f_send, f_recv, r_send, r_recv, e_send, e_recv,
 ):
     n_gx, n_ta, n_gy = sizes
     quad, deriv = gll_tables()[1:]
-    deriv = [[float(v) for v in row] for row in deriv]
+    plus = [[float(deriv[a, b] + deriv[a, 5 - b]) / 2.0 for b in range(3)] for a in range(3)]
+    minus = [[float(deriv[a, b] - deriv[a, 5 - b]) / 2.0 for b in range(3)] for a in range(3)]
     wy = [float(2.0 * quad[0])] + [float(quad[b]) for b in range(1, 5)]
     gx, ta, gy = lax.axis_index("gx"), lax.axis_index("ta"), lax.axis_index("gy")
     after, before = lax.rem(ta + 1, n_ta), lax.rem(ta + n_ta - 1, n_ta)
@@ -229,6 +229,18 @@
     sides = ((gx > 0, gx - 1), (gx < n_gx - 1, gx + 1))
     px = init_ref.shape[2]
 
+    loads = {}
+    pairs = (
+        (cond_hbm, cond_ref), (gather_hbm, gather_ref), (init_hbm, init_ref),
+        (guess_hbm, guess_ref), (cap_hbm, cap_ref), (forward_hbm, forward_ref),
+        (back_hbm, back_ref), (scatter_hbm, scatter_ref), (weight_hbm, weight_ref),
+        (face_hbm, face_ref),
+    )
+    for k, (source, target) in enumerate(pairs):
+        loads[k] = pltpu.make_async_copy(source, target, load_sem.at[k])
+
+    for load in loads.values():
+        load.start()
     barrier = pltpu.get_barrier_semaphore()
 
     def greet(x, t, y):
@@ -250,6 +262,8 @@
             for there, x in sides:
                 pl.when(there)(functools.partial(greet, x, after, p))
 
+    for k in (1, 2, 3):
+        loads[k].wait()
     gather = gather_ref[...]
     first = ta == 0
     starts_first = jnp.logical_or(first, ta == n_ta - 1)
@@ -260,9 +274,13 @@
             [jnp.where(there, fresh[b], guess[b]) for b in range(5)], axis=1
         )
 
+    loads[0].wait()
     packs[0] = exact(gather, jnp.concatenate(wide_rows(cond_ref), axis=1))
-    packs[1] = exact(gather, jnp.concatenate(wide_rows(cap_ref), axis=1))
-    packs[2] = exact(gather, chosen(starts_first))
+    packs[1] = exact(gather, chosen(starts_first))
+    loads[4].wait()
+    packs[2] = exact(gather, jnp.concatenate(wide_rows(cap_ref), axis=1))
+    for k in range(5, len(pairs)):
+        loads[k].wait()
     own_faces = exact(gather[:16], chosen(first))
     faces_out[0] = own_faces[:8]
     faces_out[1] = own_faces[8:]
@@ -322,26 +340,29 @@
         for p in range(n_gy):
             wait_inputs(0, p)
             kappa = inputs[0, p]
-            spread_out = product(spread_ref[...], extended(kappa))
+            spread_out = product(forward_ref[1].astype(jnp.bfloat16), extended(kappa))
             for b in range(5):
                 flux_x[p, :, plane(b)] = spread_out[:, plane(b)] * wy[b]
                 flux_y[p, :, plane(b)] = kappa[:, plane(b)] * weight * float(quad[b])
         for p in range(n_gy):
             wait_inputs(1, p)
+            field[0, p] = inputs[1, p]
+            field[1, p] = inputs[1, p]
+            drive[p] = jnp.zeros(drive.shape[1:], jnp.float32)
+
+        def set_inverse(p):
+            wait_inputs(2, p)
             for b in range(5):
-                inv[p, :, plane(b)] = (step_len / wy[b]) / (inputs[1, p, :, plane(b)] * weight)
-        for p in range(n_gy):
-            wait_inputs(2, p)
-            field[0, p] = inputs[2, p]
-            field[1, p] = inputs[2, p]
-            drive[p] = jnp.zeros(drive.shape[1:], jnp.float32)
+                inv[p, :, plane(b)] = (step_len / wy[b]) / (inputs[2, p, :, plane(b)] * weight)
 
         sections = sec_ref[0]
 
         def coefficient(j, k):
-            value = table_ref[0, 3 * j + k]
-            for s in range(1, SMAX - SMIN + 1):
-                value = jnp.where(sections == SMIN + s, table_ref[s, 3 * j + k], value)
+            value = jnp.float32(0.0)
+            for count in range(SMIN, SMAX + 1):
+                for at, row in enumerate(rkc_table(count)):
+                    here = jnp.logical_and(sections == count, j == at)
+                    value = jnp.where(here, jnp.float32(row[k]), value)
             return value
 
         def combine(terms):
@@ -350,9 +371,11 @@
                 total = total + term
             return total
 
-        def stage(j, carry):
-            now = lax.rem(j, 2)
+        def stage(j, carry, ready=None, done=None):
+            now = j % 2
             later = 1 - now
+            forward = forward_ref[0].astype(jnp.bfloat16)
+            backward = back_ref[...].astype(jnp.bfloat16)
             mu, nu, tilde = (coefficient(j, k) for k in range(3))
             for p in range(n_gy):
                 behind = (p + 1) % n_gy
@@ -360,21 +383,29 @@
                 u.append(field[now, behind, :, plane(0)])
                 weights = [flux_y[p, :, plane(b)] for b in range(5)]
                 weights.append(flux_y[behind, :, plane(0)])
-                flux = [
-                    weights[a] * combine([deriv[a][b] * u[b] for b in range(6)])
-                    for a in range(6)
-                ]
+                sums = [u[b] + u[5 - b] for b in range(3)]
+                gaps = [u[b] - u[5 - b] for b in range(3)]
+                even = [combine([plus[a][b] * sums[b] for b in range(3)]) for a in range(3)]
+                odd = [combine([minus[a][b] * gaps[b] for b in range(3)]) for a in range(3)]
+                low = [weights[a] * (odd[a] + even[a]) for a in range(3)]
+                high = [weights[5 - a] * (odd[a] - even[a]) for a in range(3)]
+                sums = [low[a] + high[a] for a in range(3)]
+                gaps = [low[a] - high[a] for a in range(3)]
+                even = [combine([plus[a][b] * gaps[a] for a in range(3)]) for b in range(3)]
+                odd = [combine([minus[a][b] * sums[a] for a in range(3)]) for b in range(3)]
                 for b in range(6):
-                    value = combine([deriv[a][b] * flux[a] for a in range(6)])
+                    value = even[b] + odd[b] if b < 3 else even[5 - b] - odd[5 - b]
                     if b < 5:
                         y_terms[p, :, plane(b)] = value
                     else:
                         spill[p] = value
             for p in range(n_gy):
+                if ready is not None:
+                    ready(p)
                 whole = field[now, p]
                 count = whole.shape[0]
-                slopes = product(slope_ref[...], extended(whole))
-                back = product(back_ref[...], slopes * flux_x[p])
+                slopes = product(forward, extended(whole))
+                back = product(backward, slopes * flux_x[p])
                 wrapped = rolled(back[count:], 1)
                 for b in range(5):
                     u = field[now, p, :, plane(b)]
@@ -390,9 +421,12 @@
                         + nu * field[later, p, :, plane(b)]
                         - tilde * (inv[p, :, plane(b)] * total)
                     )
+                if done is not None:
+                    done(p)
             return carry
 
-        lax.fori_loop(0, SMAX, stage, 0)
+        stage(0, 0, ready=set_inverse)
+        lax.fori_loop(1, SMAX, stage, 0)
 
         for side in range(2):
             there = sides[side][0]
@@ -411,7 +445,7 @@
 
         @pl.when(ta == n_ta - 1)
         def _():
-            field[0] = inputs[2]
+            field[0] = inputs[1]
 
         for p in range(n_gy):
             field[1, p] = field[0, p]
@@ -427,10 +461,8 @@
                 for p in range(n_gy):
                     robin_copy(side, p).start()
 
-        lax.fori_loop(0, SMAX, stage, 0)
-
-        for p in range(n_gy):
-            end_copy(p).start()
+        lax.fori_loop(0, SMAX - 1, stage, 0)
+        stage(SMAX - 1, 0, done=lambda p: end_copy(p).start())
 
     @pl.when(jnp.logical_not(is_hub))
     def _():
@@ -477,11 +509,12 @@
         px = initial_field.shape[0]
         tables = constants(px)
         count = len(row_order(px))
-        slope_rows = tables[0].shape[0]
+        slope_rows = tables[0].shape[1]
         wide = 5 * LANES
         f32 = jnp.float32
         vmem = pl.BlockSpec(memory_space=pltpu.VMEM)
         smem = pl.BlockSpec(memory_space=pltpu.SMEM)
+        hbm = pl.BlockSpec(memory_space=pltpu.HBM)
         dma = pltpu.SemaphoreType.DMA
         moved = [
             jnp.transpose(a, (1, 2, 0, 3))
@@ -500,15 +533,18 @@
                 jax.ShapeDtypeStruct(opening_guess.shape, f32),
                 jax.ShapeDtypeStruct((1, 2, 1) + initial_field.shape[1:], f32),
             ),
-            in_specs=[vmem] * 4 + [smem] + [vmem] * 7 + [smem],
+            in_specs=[hbm] * 4 + [smem] + [hbm] * len(tables),
             out_specs=(vmem, vmem),
-            scratch_shapes=[pltpu.VMEM(shape, f32) for shape in shapes]
+            scratch_shapes=[pltpu.VMEM(a.shape, f32) for a in moved]
+            + [pltpu.VMEM(t.shape, t.dtype) for t in tables]
+            + [dma((4 + len(tables),))]
+            + [pltpu.VMEM(shape, f32) for shape in shapes]
             + [
                 dma((3,)), dma((3, n_gy)), dma((2,)), dma((2, n_gy)),
                 dma((2, n_gy)), dma((2,)), dma((n_gy,)), dma,
             ],
             compiler_params=pltpu.CompilerParams(
-                collective_id=0, has_side_effects=True, vmem_limit_bytes=32 * 1024 * 1024
+                collective_id=0, has_side_effects=True, vmem_limit_bytes=63 * 1024 * 1024
             ),
         )(*moved, section_count, *[jnp.asarray(t) for t in tables])
 

time: 43.9 us -> 38.3 us (0.87)
  local copies, waits for them, and re-layouts: 8.04 us -> 4 us
  Pallas kernels: 34 us -> 32.7 us
    unnamed x23 -> x3, local copies, waits for them, and re-layouts: 6.6 us -> 1.61 us
    pallas_call x1, Pallas kernels: 34 us -> 32.7 us  [local(): pl.pallas_call(functools.partial(kernel, sizes, step_size()), out_shape=(...]
    pallas_call x2, local copies, waits for them, and re-layouts: 1.44 us -> 2.39 us  [local(): pl.pallas_call(functools.partial(kernel, sizes, step_size()), out_shape=(...]
where the time goes in v3:
time: 38.3 us; the launch traced here: 38 us
  Pallas kernels  32.7 us (85%)
  local copies, waits for them, and re-layouts  4 us (10%)
  between operations  1.29 us (3%)
    pallas_call x1, Pallas kernels, local(): pl.pallas_call(functools.partial(kernel, sizes, step_size()), out_shape=(...  32.7 us
    pallas_call x2, local copies, waits for them, and re-layouts, local(): pl.pallas_call(functools.partial(kernel, sizes, step_size()), out_shape=(...  2.39 us
    unnamed x3, local copies, waits for them, and re-layouts  1.61 us

profile of v3, /device:TPU:0, one launch (start us, length us, event | category | flops | bytes accessed | tf_op | source)
XLA Modules:
  0.0 38.0 jit_solution(3398017905357334507)
XLA Ops:
  1.3 1.6 %copy.17 = f32[1,11,5,5,128]{4,1,3,2,0:T(8,128)} copy(f32[1,11,5,5,128]{4,0,3,2,1:T(1,128)} %param.12) | data formatting | bytes 281600 | tf_op args[1]
  2.9 32.7 %shard_map.122 = (f32[1,11,5,5,128]{4,3,2,1,0:T(8,128)}, f32[1,2,1,5,5,128]{5,4,3,2,1,0:T(8,128)}) custom-call(f32[5,5,11,128]{3,2,1,0:T(8,128)} %bitcast.9, f32[5,5,11,128]{3,2,1,0:T(8,128)} %bitcast.8, f32[5,5,11,128]{3,2,1,0:T(8,128)} %bitcast.10, f32[5,5,11,128]{3,2,1,0:T(8,128)} %bitcast.11, s32[1]{0:T(128)S(6)} %copy.18.sec_ref, ...), custom_call_target="tpu_custom_call" | custom-call | tf_op jit(solution)/shard_map/pallas_call | solution.py:530
  35.6 0.0 copy-start
  35.6 1.8 %copy.14 = f32[1,11,5,5,128]{4,0,3,2,1:T(1,128)} copy(f32[1,11,5,5,128]{4,3,2,1,0:T(8,128)} %get-tuple-element.2) | data formatting | bytes 281600 | tf_op jit(solution)/shard_map/pallas_call | solution.py:530
  37.4 0.0 copy-done
  37.4 0.6 %copy.15 = f32[1,2,1,5,5,128]{5,2,4,3,1,0:T(1,128)} copy(f32[1,2,1,5,5,128]{5,4,3,2,1,0:T(8,128)S(1)} %copy-done) | data formatting | bytes 51200 | tf_op jit(solution)/shard_map/pallas_call | solution.py:530
Async XLA Ops:
  35.6 1.8 %copy-start = (f32[1,2,1,5,5,128]{5,4,3,2,1,0:T(8,128)S(1)}, f32[1,2,1,5,5,128]{5,4,3,2,1,0:T(8,128)}, u32[]{:S(2)}) copy-start(f32[1,2,1,5,5,128]{5,4,3,2,1,0:T(8,128)} %get-tuple-element.3) | copy-start | bytes 76804

commit v4 on v3

--- a/solution.py
+++ b/solution.py
@@ -276,15 +276,6 @@
 
     loads[0].wait()
     packs[0] = exact(gather, jnp.concatenate(wide_rows(cond_ref), axis=1))
-    packs[1] = exact(gather, chosen(starts_first))
-    loads[4].wait()
-    packs[2] = exact(gather, jnp.concatenate(wide_rows(cap_ref), axis=1))
-    for k in range(5, len(pairs)):
-        loads[k].wait()
-    own_faces = exact(gather[:16], chosen(first))
-    faces_out[0] = own_faces[:8]
-    faces_out[1] = own_faces[8:]
-
     pl.semaphore_wait(
         barrier,
         2 + neighbours + is_hub.astype(jnp.int32) * (2 * n_gy - 2 + n_gy * neighbours),
@@ -317,10 +308,17 @@
             device_id={"gx": sides[side][1], "ta": after, "gy": p}, device_id_type=MESH,
         )
 
-    @pl.when(jnp.logical_not(is_hub))
-    def _():
-        for k in range(3):
-            input_copy(k).start()
+    pl.when(jnp.logical_not(is_hub))(input_copy(0).start)
+    packs[1] = exact(gather, chosen(starts_first))
+    pl.when(jnp.logical_not(is_hub))(input_copy(1).start)
+    loads[4].wait()
+    packs[2] = exact(gather, jnp.concatenate(wide_rows(cap_ref), axis=1))
+    pl.when(jnp.logical_not(is_hub))(input_copy(2).start)
+    for k in range(5, len(pairs)):
+        loads[k].wait()
+    own_faces = exact(gather[:16], chosen(first))
+    faces_out[0] = own_faces[:8]
+    faces_out[1] = own_faces[8:]
 
     for side in range(2):
         pl.when(sides[side][0])(face_copy(side).start)
@@ -426,7 +424,8 @@
             return carry
 
         stage(0, 0, ready=set_inverse)
-        lax.fori_loop(1, SMAX, stage, 0)
+        for j in range(1, SMAX):
+            stage(j, 0)
 
         for side in range(2):
             there = sides[side][0]
@@ -461,7 +460,8 @@
                 for p in range(n_gy):
                     robin_copy(side, p).start()
 
-        lax.fori_loop(0, SMAX - 1, stage, 0)
+        for j in range(SMAX - 1):
+            stage(j, 0)
         stage(SMAX - 1, 0, done=lambda p: end_copy(p).start())
 
     @pl.when(jnp.logical_not(is_hub))

time: 38.3 us -> 37.7 us (0.984)
  Pallas kernels: 32.7 us -> 32 us
    pallas_call x1, Pallas kernels: 32.7 us -> 32 us  [local(): pl.pallas_call(functools.partial(kernel, sizes, step_size()), out_shape=(...]
where the time goes in v4:
time: 37.7 us; the launch traced here: 37.3 us
  Pallas kernels  32 us (85%)
  local copies, waits for them, and re-layouts  4 us (11%)
  between operations  1.29 us (3%)
    pallas_call x1, Pallas kernels, local(): pl.pallas_call(functools.partial(kernel, sizes, step_size()), out_shape=(...  32 us
    pallas_call x2, local copies, waits for them, and re-layouts, local(): pl.pallas_call(functools.partial(kernel, sizes, step_size()), out_shape=(...  2.39 us
    unnamed x3, local copies, waits for them, and re-layouts  1.61 us

profile of v4, /device:TPU:0, one launch (start us, length us, event | category | flops | bytes accessed | tf_op | source)
XLA Modules:
  0.0 37.3 jit_solution(7550371453444443875)
XLA Ops:
  1.3 1.6 %copy.17 = f32[1,11,5,5,128]{4,1,3,2,0:T(8,128)} copy(f32[1,11,5,5,128]{4,0,3,2,1:T(1,128)} %param.12) | data formatting | bytes 281600 | tf_op args[1]
  2.9 32.0 %shard_map.122 = (f32[1,11,5,5,128]{4,3,2,1,0:T(8,128)}, f32[1,2,1,5,5,128]{5,4,3,2,1,0:T(8,128)}) custom-call(f32[5,5,11,128]{3,2,1,0:T(8,128)} %bitcast.9, f32[5,5,11,128]{3,2,1,0:T(8,128)} %bitcast.8, f32[5,5,11,128]{3,2,1,0:T(8,128)} %bitcast.10, f32[5,5,11,128]{3,2,1,0:T(8,128)} %bitcast.11, s32[1]{0:T(128)S(6)} %copy.18.sec_ref, ...), custom_call_target="tpu_custom_call" | custom-call | tf_op jit(solution)/shard_map/pallas_call | solution.py:530
  34.9 0.0 copy-start
  34.9 1.8 %copy.14 = f32[1,11,5,5,128]{4,0,3,2,1:T(1,128)} copy(f32[1,11,5,5,128]{4,3,2,1,0:T(8,128)} %get-tuple-element.2) | data formatting | bytes 281600 | tf_op jit(solution)/shard_map/pallas_call | solution.py:530
  36.6 0.0 copy-done
  36.6 0.6 %copy.15 = f32[1,2,1,5,5,128]{5,2,4,3,1,0:T(1,128)} copy(f32[1,2,1,5,5,128]{5,4,3,2,1,0:T(8,128)S(1)} %copy-done) | data formatting | bytes 51200 | tf_op jit(solution)/shard_map/pallas_call | solution.py:530
Async XLA Ops:
  34.9 1.8 %copy-start = (f32[1,2,1,5,5,128]{5,4,3,2,1,0:T(8,128)S(1)}, f32[1,2,1,5,5,128]{5,4,3,2,1,0:T(8,128)}, u32[]{:S(2)}) copy-start(f32[1,2,1,5,5,128]{5,4,3,2,1,0:T(8,128)} %get-tuple-element.3) | copy-start | bytes 76804
